TPU v7x, 128 devices: a whole 4x4x4 slice. The times are simulated.
128 devices in a mesh: pool: 2 (over core), dev: 64 (over x, z, y).
Axes of the slice: x: 4, y: 4, z: 4, core: 2. Of those that a mesh axis runs over, the one named last changes fastest.
Arguments:
- hidden: bfloat16 [2048, 4096], P(('pool', 'dev')), may hold values from -6 to 6
- queries: bfloat16 [2048, 8192], P(('pool', 'dev')), may hold values from -160 to 160
- k_cache: bfloat16 [2048, 128, 512], P(('pool', 'dev')), may hold values from -6 to 6
- v_cache: bfloat16 [2048, 128, 512], P(('pool', 'dev')), may hold values from -6 to 6
- o_weight: bfloat16 [8192, 4096], P('dev'), may hold values from -0.125 to 0.125
- norm_gain: bfloat16 [4096], replicated, may hold values from 0.25 to 1.75
- router_weight: bfloat16 [4096, 128], replicated, may hold values from -0.1875 to 0.1875
- w_gate: bfloat16 [128, 4096, 768], P(('pool', 'dev')), may hold values from -0.09375 to 0.09375
- w_up: bfloat16 [128, 4096, 768], P(('pool', 'dev')), may hold values from -0.09375 to 0.09375
- w_down: bfloat16 [128, 768, 4096], P(('pool', 'dev')), may hold values from -0.4375 to 0.4375
- routes: int32 [2048, 8], P(('pool', 'dev')), may hold values from 0 to 127, all different within a row; in each aligned block of 16 rows (0 to 15, 16 to 31, ...) at most 2 rows name the same one
Outputs:
- layer_out: bfloat16 [2048, 4096], P(('pool', 'dev'))
Inputs may be any that keep to these rules, and one draw needn't show every extreme that they name: `routes`: each token names 8 different experts; among the 16 tokens of one device no expert is named more than 2 times.
All inputs are finite; a program needn't handle non-finite values.
Results may differ from a plain program's by a relative error of at most 0.023.
Values may be sent and summed in bfloat16 or wider, within the bound.
A program may use at most 128 MiB of HBM per device.

v0:
```python
import math

import jax
import jax.numpy as jnp
from jax import lax
from jax.sharding import PartitionSpec as P

QH = 64
KVH = 4
HD = 128
TOPK = 8


def expert_rows(inputs, gate_weight, up_weight, down_weight):
    gate_value = jnp.dot(inputs, gate_weight, preferred_element_type=jnp.float32)
    up_value = jnp.dot(inputs, up_weight, preferred_element_type=jnp.float32)
    activated = (jax.nn.silu(gate_value) * up_value).astype(jnp.bfloat16)
    return jnp.dot(activated, down_weight, preferred_element_type=jnp.float32).astype(jnp.bfloat16)


def expert_block(received, gate_weight, up_weight, down_weight):
    flat_rows = received.reshape(-1, received.shape[-1])
    return expert_rows(flat_rows, gate_weight, up_weight, down_weight).reshape(received.shape)


def shards(
    hidden,
    queries,
    k_cache,
    v_cache,
    o_weight,
    norm_gain,
    router_weight,
    w_gate,
    w_up,
    w_down,
    routes,
):
    tok_rows = hidden.shape[0]
    model_width = hidden.shape[1]
    per_group = QH // KVH
    query_b = queries.reshape(tok_rows, KVH, per_group, HD)
    key_b = k_cache.reshape(tok_rows, -1, KVH, HD)
    value_b = v_cache.reshape(tok_rows, -1, KVH, HD)
    scores = jnp.einsum(
        "tgqd,tcgd->tgqc", query_b, key_b, preferred_element_type=jnp.float32
    ) / math.sqrt(HD)
    attn_probs = jax.nn.softmax(scores, axis=-1).astype(jnp.bfloat16)
    attended = jnp.einsum(
        "tgqc,tcgd->tgqd", attn_probs, value_b, preferred_element_type=jnp.float32
    )
    attended = attended.astype(jnp.bfloat16).reshape(tok_rows, QH, HD)
    by_head = lax.all_to_all(attended, "dev", split_axis=1, concat_axis=0, tiled=True)
    head_rows = by_head.reshape(by_head.shape[0], -1)
    project = lax.psum_scatter(
        jnp.dot(head_rows, o_weight, preferred_element_type=jnp.float32),
        "dev",
        scatter_dimension=0,
        tiled=True,
    )
    residual = (hidden.astype(jnp.float32) + project).astype(jnp.bfloat16)
    resid_f = residual.astype(jnp.float32)
    mean_square = jnp.mean(resid_f * resid_f, axis=-1, keepdims=True)
    normed = (resid_f * lax.rsqrt(mean_square + 1e-06) * norm_gain.astype(jnp.float32)).astype(
        jnp.bfloat16
    )
    logits = jnp.dot(normed, router_weight, preferred_element_type=jnp.float32)
    chosen = jnp.take_along_axis(logits, routes, axis=1)
    weights = jax.nn.softmax(chosen, axis=-1)
    experts_all = router_weight.shape[1]
    slot_count = max(2, 2 * tok_rows * TOPK // experts_all)
    flat_ids = routes.reshape(-1)
    onehot = (flat_ids[:, None] == jnp.arange(experts_all)[None, :]).astype(jnp.int32)
    earlier = jnp.cumsum(onehot, axis=0) - onehot
    slot_rank = jnp.sum(earlier * onehot, axis=1)
    position = flat_ids * slot_count + slot_rank
    picker = (jnp.arange(experts_all * slot_count)[:, None] == position[None, :]).astype(jnp.int32)
    select = jnp.sum(picker.reshape(experts_all * slot_count, tok_rows, -1), axis=2).astype(
        jnp.bfloat16
    )
    outgoing = jnp.dot(select, normed, preferred_element_type=jnp.float32).astype(jnp.bfloat16)
    outgoing = outgoing.reshape(experts_all, slot_count, model_width)
    gate_weight = w_gate[0]
    up_weight = w_up[0]
    down_weight = w_down[0]
    produced = expert_block(
        lax.all_to_all(outgoing, ("pool", "dev"), split_axis=0, concat_axis=0, tiled=True),
        gate_weight,
        up_weight,
        down_weight,
    )
    returned = lax.all_to_all(produced, ("pool", "dev"), split_axis=0, concat_axis=0, tiled=True)
    returned = returned.reshape(experts_all * slot_count, model_width)
    gathered = returned[position].astype(jnp.float32).reshape(tok_rows, -1, model_width)
    mixture = jnp.sum(weights[:, :, None] * gathered, axis=1)
    return (resid_f + mixture).astype(jnp.bfloat16)


def solution(mesh):
    placed = (
        P(("pool", "dev"), None),
        P(("pool", "dev"), None),
        P(("pool", "dev"), None, None),
        P(("pool", "dev"), None, None),
        P("dev", None),
        P(),
        P(),
        P(("pool", "dev"), None, None),
        P(("pool", "dev"), None, None),
        P(("pool", "dev"), None, None),
        P(("pool", "dev"), None),
    )
    return jax.shard_map(
        shards, mesh=mesh, in_specs=placed, out_specs=P(("pool", "dev"), None), check_vma=False
    )
```

profile of v0, /device:TPU:1, one launch (start us, length us, event | category | flops | bytes accessed | tf_op | source)
XLA Modules:
  0.0 552.5 jit_solution(17822184240750523261)
XLA Ops:
  6.5 0.0 copy-start
  6.5 0.0 reduce-scatter.2.cloned.1.call-start
  6.5 1.1 copy.37
  7.7 0.5 copy-done
  8.2 1.2 fusion.25
  9.4 0.4 fusion.51
  9.8 3.4 fusion.28
  13.2 0.2 copy.29
  13.4 21.1 %all_to_all.25 = bf16[16,64,128]{2,0,1:T(8,128)(2,1)S(1)} all-to-all(bf16[16,64,128]{2,0,1:T(8,128)(2,1)S(1)} %copy.29), channel_id=1, replica_groups=mesh['pool'=2,'dev'=64] {'dev'}, dimensions={1} | all-to-all | bytes 524288 | tf_op jit(solution)/shard_map/all_to_all | solution.py:53
  34.5 9.3 %fusion.52 = f32[1024,4096]{1,0:T(8,128)} fusion(bf16[1024,128]{1,0:T(8,128)(2,1)S(1)} %bitcast.65, bf16[128,4096]{1,0:T(8,128)(2,1)} %param.15), kind=kOutput, calls=%fused_computation.60 | convolution fusion | flops 1073741824 | bytes 18087936 | tf_op jit(solution)/shard_map/dot_general | solution.py:56
  43.8 0.0 copy-start.3
  43.8 0.0 copy-start.2
  43.8 0.0 copy-start.1
  43.8 0.0 reduce-scatter.2.cloned.1.call-update
  43.8 0.7 copy-done.3
  44.5 0.0 copy-done.2
  44.5 0.1 copy.33
  44.5 0.1 eq.30
  44.6 0.1 fusion.39
  44.7 0.2 reduce_window_sum.11
  44.9 0.2 select_reduce_fusion
  45.1 0.1 reduce_sum.62
  45.2 0.1 convert_reduce_fusion
  45.3 334.8 %reduce-scatter.2.cloned.1.call-done = f32[16,4096]{1,0:T(8,128)} async-done(((f32[1024,4096]{1,0:T(8,128)}), f32[16,4096]{1,0:T(8,128)}) %reduce-scatter.2.cloned.1.call-update) | async-done | bytes 262160 | tf_op jit(solution)/shard_map/reduce_scatter | solution.py:55
  380.1 0.0 copy-done.1
  380.1 1.1 fusion.34
  381.3 2.1 convolution_convert_fusion
  383.3 4.4 reshape.125
  387.7 85.9 %all_to_all.26 = bf16[128,2,4096]{2,1,0:T(2,128)(2,1)} all-to-all(bf16[128,2,4096]{2,1,0:T(2,128)(2,1)} %reshape.125), channel_id=1, replica_groups=mesh['pool'=2,'dev'=64] {'pool','dev'}, dimensions={0} | all-to-all | bytes 4194304 | tf_op jit(solution)/shard_map/all_to_all | solution.py:87
  473.6 4.1 reshape.126
  477.8 6.1 %fusion.5 = f32[256,768]{1,0:T(8,128)} fusion(bf16[256,4096]{1,0:T(8,128)(2,1)} %reshape.126, bf16[1,4096,768]{2,1,0:T(8,128)(2,1)} %param.18), kind=kOutput, calls=%fused_computation.7 | convolution fusion | flops 1610612736 | bytes 9175040 | tf_op jit(solution)/shard_map/dot_general | solution.py:15
  483.8 11.3 %fusion.7 = bf16[256,4096]{1,0:T(8,128)(2,1)} fusion(bf16[1,768,4096]{2,1,0:T(8,128)(2,1)} %param.20, bf16[256,4096]{1,0:T(8,128)(2,1)} %reshape.126, bf16[1,4096,768]{2,1,0:T(8,128)(2,1)} %param.19, f32[256,768]{1,0:T(8,128)} %fusion.5), kind=kOutput, calls=%fused_computation.10 | convolution fusion | flops 3223453696 | bytes 17563648 | tf_op jit(solution)/shard_map/dot_general | solution.py:18
  495.1 4.4 reshape.127
  499.5 6.3 %all-to-all-start.2 = ((bf16[128,2,4096]{2,1,0:T(2,128)(2,1)}), bf16[128,2,4096]{2,1,0:T(2,128)(2,1)}, u32[]{:S(2)}, u32[]{:S(2)}) async-start(bf16[128,2,4096]{2,1,0:T(2,128)(2,1)} %reshape.127), calls=%async_computation.3 | async-start | bytes 4194304 | tf_op jit(solution)/shard_map/all_to_all | solution.py:92
  505.8 0.1 copy.30
  505.9 0.1 reshape.138
  506.0 0.1 mul.68
  506.1 1.5 fusion.41
  507.7 1.3 gather_fusion.1
  508.9 0.1 reshape.141
  509.0 0.1 copy.31
  509.1 0.1 copy.32
  509.2 26.8 %all-to-all-done.2 = bf16[128,2,4096]{2,1,0:T(2,128)(2,1)} async-done(((bf16[128,2,4096]{2,1,0:T(2,128)(2,1)}), bf16[128,2,4096]{2,1,0:T(2,128)(2,1)}, u32[]{:S(2)}, u32[]{:S(2)}) %all-to-all-start.2) | async-done | bytes 2097184 | tf_op jit(solution)/shard_map/all_to_all | solution.py:92
  536.0 4.1 reshape.128
  540.1 4.1 gather_fusion
  544.2 0.8 fusion.16
  545.0 0.7 fusion.37
  (9 shorter events, 0.1 us)
Async XLA Ops:
  6.5 1.7 copy-start
  6.5 373.6 %reduce-scatter.2.cloned.1.call-start = ((), (), s32[]{:S(2)}) async-start(), calls=%async_computation.4 | async-start | bytes 17039360 | tf_op jit(solution)/shard_map/reduce_scatter | solution.py:55
  43.8 0.7 copy-start.3
  43.8 0.7 copy-start.2
  43.8 336.4 %copy-start.1 = (bf16[16,4096]{1,0:T(8,128)(2,1)S(1)}, bf16[16,4096]{1,0:T(8,128)(2,1)}, u32[]{:S(2)}) copy-start(bf16[16,4096]{1,0:T(8,128)(2,1)} %param.11) | copy-start | bytes 393220
  499.5 36.5 %all-to-all-start.2 = ((bf16[128,2,4096]{2,1,0:T(2,128)(2,1)}), bf16[128,2,4096]{2,1,0:T(2,128)(2,1)}, u32[]{:S(2)}, u32[]{:S(2)}) async-start(bf16[128,2,4096]{2,1,0:T(2,128)(2,1)} %reshape.127), calls=%async_computation.3 | async-start | bytes 4194304 | tf_op jit(solution)/shard_map/all_to_all | solution.py:92
Sparse Core Ops, SparseCore 0:
  43.9 336.1 reduce-scatter.1
where the time goes:
time: 553 us
  waiting for transfers between devices  362 us (65%)
  blocking collectives  107 us (19%)
  matrix products  34.9 us (6%)
  local copies, waits for them, and re-layouts  25.6 us (5%)
  between operations  13.5 us (2%)
  starting transfers between devices  6.31 us (1%)
    reduce_scatter x1, waiting for transfers between devices, shards(): lax.psum_scatter(jnp.dot(head_rows, o_weight, preferred_element_type=jnp....  335 us
    all_to_all x1, blocking collectives, shards(): lax.all_to_all(outgoing, ('pool', 'dev'), split_axis=0, concat_axis=0, ti...  85.9 us
    all_to_all x1, waiting for transfers between devices, shards(): lax.all_to_all(produced, ('pool', 'dev'), split_axis=0, concat_axis=0, ti...  26.8 us
    all_to_all x1, blocking collectives, shards(): lax.all_to_all(attended, 'dev', split_axis=1, concat_axis=0, tiled=True)  21.1 us
    dot_general x1, matrix products, expert_rows(): jnp.dot(activated, down_weight, preferred_element_type=jnp.float32)  11.3 us
  transfers between devices with their start and end apart: 2, of which 2 were waited for; matrix products, arithmetic and copies ran while one was open for 1% of the time, Pallas kernels for 0%

commit v1 on v0

--- a/solution.py
+++ b/solution.py
@@ -9,6 +9,10 @@
 KVH = 4
 HD = 128
 TOPK = 8
+LINE = 4
+PLANE = 16
+LINES = [[LINE * i + j for j in range(LINE)] for i in range(PLANE)]
+PLANES = [[LINE * i + j for i in range(PLANE)] for j in range(LINE)]
 
 
 def expert_rows(inputs, gate_weight, up_weight, down_weight):
@@ -49,15 +53,22 @@
     attended = jnp.einsum(
         "tgqc,tcgd->tgqd", attn_probs, value_b, preferred_element_type=jnp.float32
     )
-    attended = attended.astype(jnp.bfloat16).reshape(tok_rows, QH, HD)
-    by_head = lax.all_to_all(attended, "dev", split_axis=1, concat_axis=0, tiled=True)
-    head_rows = by_head.reshape(by_head.shape[0], -1)
-    project = lax.psum_scatter(
-        jnp.dot(head_rows, o_weight, preferred_element_type=jnp.float32),
+    attended = attended.astype(jnp.bfloat16).reshape(tok_rows, PLANE, -1)
+    by_head = lax.all_to_all(
+        attended, "dev", split_axis=1, concat_axis=0, tiled=True, axis_index_groups=PLANES
+    )
+    head_rows = by_head.reshape(PLANE * tok_rows, -1)
+    wide = lax.all_gather(o_weight, "dev", axis_index_groups=LINES, tiled=True)
+    partial = jnp.dot(head_rows, wide, preferred_element_type=jnp.float32).astype(jnp.bfloat16)
+    shares = lax.all_to_all(
+        partial.reshape(PLANE, tok_rows, -1),
         "dev",
-        scatter_dimension=0,
+        split_axis=0,
+        concat_axis=0,
         tiled=True,
+        axis_index_groups=PLANES,
     )
+    project = jnp.sum(shares.astype(jnp.float32), axis=0)
     residual = (hidden.astype(jnp.float32) + project).astype(jnp.bfloat16)
     resid_f = residual.astype(jnp.float32)
     mean_square = jnp.mean(resid_f * resid_f, axis=-1, keepdims=True)

time: 553 us -> 227 us (0.41)
  waiting for transfers between devices: 362 us -> 85.8 us
  blocking collectives: 107 us -> 54.4 us
  starting transfers between devices: 6.31 us -> 13.2 us
    reduce_scatter x1 -> x0, waiting for transfers between devices: 335 us -> none  [shards(): lax.psum_scatter(jnp.dot(head_rows, o_weight, preferred_element_type=jnp....]
    all_to_all x1, blocking collectives: 85.9 us -> 38.7 us  [shards(): lax.all_to_all(outgoing, ('pool', 'dev'), split_axis=0, concat_axis=0, ti...]
    all_gather x0 -> x1, waiting for transfers between devices: none -> 31.2 us  [shards(): wide = lax.all_gather(o_weight, 'dev', axis_index_groups=LINES, tiled=True)]
    all_to_all x0 -> x1, waiting for transfers between devices: none -> 27.1 us  [shards(): lax.all_to_all(partial.reshape(PLANE, tok_rows, -1), 'dev', split_axis=0,...]
    all_to_all x0 -> x1, starting transfers between devices: none -> 6.85 us  [shards(): lax.all_to_all(partial.reshape(PLANE, tok_rows, -1), 'dev', split_axis=0,...]
  transfers between devices with their start and end apart: 2 -> 3, of which waited for: 2 -> 3; matrix products, arithmetic and copies ran while one was open for 1% -> 5% of each run, Pallas kernels for 0% -> 0%
where the time goes in v1:
time: 227 us; the launch traced here: 226 us
  waiting for transfers between devices  85.8 us (38%)
  blocking collectives  54.4 us (24%)
  matrix products  30.4 us (13%)
  local copies, waits for them, and re-layouts  24.4 us (11%)
  between operations  13.6 us (6%)
  starting transfers between devices  13.2 us (6%)
  other arithmetic  4.6 us (2%)
    all_to_all x1, blocking collectives, shards(): lax.all_to_all(outgoing, ('pool', 'dev'), split_axis=0, concat_axis=0, ti...  38.7 us
    all_gather x1, waiting for transfers between devices, shards(): wide = lax.all_gather(o_weight, 'dev', axis_index_groups=LINES, tiled=True)  31.2 us
    all_to_all x1, waiting for transfers between devices, shards(): lax.all_to_all(partial.reshape(PLANE, tok_rows, -1), 'dev', split_axis=0,...  27.1 us
    all_to_all x1, waiting for transfers between devices, shards(): lax.all_to_all(produced, ('pool', 'dev'), split_axis=0, concat_axis=0, ti...  26.8 us
    all_to_all x1, blocking collectives, shards(): lax.all_to_all(attended, 'dev', split_axis=1, concat_axis=0, tiled=True,...  15.7 us
    dot_general x1, matrix products, expert_rows(): jnp.dot(activated, down_weight, preferred_element_type=jnp.float32)  11.3 us
    all_to_all x1, starting transfers between devices, shards(): lax.all_to_all(partial.reshape(PLANE, tok_rows, -1), 'dev', split_axis=0,...  6.85 us
    all_to_all x1, starting transfers between devices, shards(): lax.all_to_all(produced, ('pool', 'dev'), split_axis=0, concat_axis=0, ti...  6.31 us
  transfers between devices with their start and end apart: 3, of which 3 were waited for; matrix products, arithmetic and copies ran while one was open for 5% of the time, Pallas kernels for 0%

profile of v1, /device:TPU:1, one launch (start us, length us, event | category | flops | bytes accessed | tf_op | source)
XLA Modules:
  0.0 226.3 jit_solution(15384103702846129851)
XLA Ops:
  6.5 0.0 copy-start
  6.5 0.0 all-gather.2.cloned.1.call-start
  6.5 0.7 all-gather.2.cloned.1.call-update
  7.3 1.0 copy.37
  8.3 0.0 copy-done
  8.3 1.2 fusion.25
  9.5 0.4 fusion.51
  9.9 3.4 %fusion.28 = bf16[16,4,16,128]{3,2,1,0:T(8,128)(2,1)S(1)} fusion(f32[16,4,16]{2,1,0:T(4,128)S(1)} %fusion.51, f32[16,4,16,128]{3,2,1,0:T(8,128)S(1)} %fusion.25, bf16[16,128,512]{2,1,0:T(8,128)(2,1)} %param.14), kind=kOutput, calls=%fused_computation.26 | convolution fusion | flops 34079872 | bytes 2887680 | tf_op jit(solution)/shard_map/tgqc,tcgd->tgqd/dot_general | solution.py:53
  13.3 0.2 reshape.125
  13.5 0.2 copy.29
  13.6 15.7 %all_to_all.30 = bf16[16,16,512]{2,0,1:T(8,128)(2,1)S(1)} all-to-all(bf16[16,16,512]{2,0,1:T(8,128)(2,1)S(1)} %copy.29), channel_id=1, replica_groups={{0,4,8,12,16,20,24,28,32,36,40,44,48,52,56,60},{1,5,9,13,17,21,25,29,33..., dimensions={1} | all-to-all | bytes 524288 | tf_op jit(solution)/shard_map/all_to_all | solution.py:57
  29.3 31.2 %all-gather.2.cloned.1.call-done = bf16[512,4096]{1,0:T(8,128)(2,1)} async-done(((bf16[128,4096]{1,0:T(8,128)(2,1)}), bf16[512,4096]{1,0:T(8,128)(2,1)}) %all-gather.2.cloned.1.call-update) | async-done | bytes 4194320 | tf_op jit(solution)/shard_map/all_gather | solution.py:61
  60.6 4.8 %convolution_convert_fusion.1 = bf16[256,4096]{1,0:T(8,128)(2,1)} fusion(bf16[256,512]{1,0:T(8,128)(2,1)S(1)} %bitcast.70, bf16[512,4096]{1,0:T(8,128)(2,1)} %all-gather.2.cloned.1.call-done), kind=kOutput, calls=%fused_computation.10 | convolution fusion | flops 1074790400 | bytes 6553600 | tf_op jit(solution)/shard_map/dot_general | solution.py:62
  65.3 6.8 %all-to-all-start.1 = ((bf16[16,16,4096]{2,1,0:T(8,128)(2,1)}), bf16[16,16,4096]{2,1,0:T(8,128)(2,1)}, u32[]{:S(2)}, u32[]{:S(2)}) async-start(bf16[16,16,4096]{2,1,0:T(8,128)(2,1)} %bitcast.67), calls=%async_computation.1 | async-start | bytes 4194304 | tf_op jit(solution)/shard_map/all_to_all | solution.py:63
  72.2 0.0 copy-done.3
  72.2 0.0 copy-start.1
  72.2 0.1 copy.33
  72.3 0.1 eq.30
  72.4 0.1 fusion.39
  72.5 0.2 reduce_window_sum.11
  72.7 0.2 select_reduce_fusion
  72.8 0.1 reduce_sum.72
  72.9 0.1 convert_reduce_fusion.1
  73.1 27.1 %all-to-all-done.1 = bf16[16,16,4096]{2,1,0:T(8,128)(2,1)} async-done(((bf16[16,16,4096]{2,1,0:T(8,128)(2,1)}), bf16[16,16,4096]{2,1,0:T(8,128)(2,1)}, u32[]{:S(2)}, u32[]{:S(2)}) %all-to-all-start.1) | async-done | bytes 2097184 | tf_op jit(solution)/shard_map/all_to_all | solution.py:63
  100.1 1.9 convert_reduce_fusion
  102.0 0.0 copy-done.1
  102.1 0.2 fusion.34
  102.2 2.1 convolution_convert_fusion
  104.3 4.4 %reshape.129 = bf16[128,2,4096]{2,1,0:T(2,128)(2,1)} reshape(bf16[256,4096]{1,0:T(8,128)(2,1)} %convolution_convert_fusion) | data formatting | bytes 4194304 | tf_op jit(solution)/shard_map/reshape | solution.py:93
  108.7 38.7 %all_to_all.31 = bf16[128,2,4096]{2,1,0:T(2,128)(2,1)} all-to-all(bf16[128,2,4096]{2,1,0:T(2,128)(2,1)} %reshape.129), channel_id=1, replica_groups=mesh['pool'=2,'dev'=64] {'pool','dev'}, dimensions={0} | all-to-all | bytes 4194304 | tf_op jit(solution)/shard_map/all_to_all | solution.py:98
  147.4 4.1 %reshape.130 = bf16[256,4096]{1,0:T(8,128)(2,1)} reshape(bf16[128,2,4096]{2,1,0:T(2,128)(2,1)} %all_to_all.31) | data formatting | bytes 4194304 | tf_op jit(solution)/shard_map/reshape | solution.py:26
  151.5 6.1 %fusion.5 = f32[256,768]{1,0:T(8,128)} fusion(bf16[256,4096]{1,0:T(8,128)(2,1)} %reshape.130, bf16[1,4096,768]{2,1,0:T(8,128)(2,1)} %param.18), kind=kOutput, calls=%fused_computation.7 | convolution fusion | flops 1610612736 | bytes 9175040 | tf_op jit(solution)/shard_map/dot_general | solution.py:19
  157.6 11.3 %fusion.7 = bf16[256,4096]{1,0:T(8,128)(2,1)} fusion(bf16[1,768,4096]{2,1,0:T(8,128)(2,1)} %param.20, bf16[256,4096]{1,0:T(8,128)(2,1)} %reshape.130, bf16[1,4096,768]{2,1,0:T(8,128)(2,1)} %param.19, f32[256,768]{1,0:T(8,128)} %fusion.5), kind=kOutput, calls=%fused_computation.11 | convolution fusion | flops 3223453696 | bytes 17563648 | tf_op jit(solution)/shard_map/dot_general | solution.py:22
  168.9 4.4 %reshape.131 = bf16[128,2,4096]{2,1,0:T(2,128)(2,1)} reshape(bf16[256,4096]{1,0:T(8,128)(2,1)} %fusion.7) | data formatting | bytes 4194304 | tf_op jit(solution)/shard_map/reshape | solution.py:27
  173.3 6.3 %all-to-all-start.3 = ((bf16[128,2,4096]{2,1,0:T(2,128)(2,1)}), bf16[128,2,4096]{2,1,0:T(2,128)(2,1)}, u32[]{:S(2)}, u32[]{:S(2)}) async-start(bf16[128,2,4096]{2,1,0:T(2,128)(2,1)} %reshape.131), calls=%async_computation.3 | async-start | bytes 4194304 | tf_op jit(solution)/shard_map/all_to_all | solution.py:103
  179.6 0.1 copy.30
  179.7 0.1 reshape.142
  179.8 0.1 mul.68
  179.9 1.5 fusion.41
  181.4 1.3 gather_fusion.1
  182.7 0.1 reshape.145
  182.8 0.1 copy.31
  182.9 0.1 copy.32
  183.0 26.8 %all-to-all-done.3 = bf16[128,2,4096]{2,1,0:T(2,128)(2,1)} async-done(((bf16[128,2,4096]{2,1,0:T(2,128)(2,1)}), bf16[128,2,4096]{2,1,0:T(2,128)(2,1)}, u32[]{:S(2)}, u32[]{:S(2)}) %all-to-all-start.3) | async-done | bytes 2097184 | tf_op jit(solution)/shard_map/all_to_all | solution.py:103
  209.8 4.1 %reshape.132 = bf16[256,4096]{1,0:T(8,128)(2,1)} reshape(bf16[128,2,4096]{2,1,0:T(2,128)(2,1)} %all-to-all-done.3) | data formatting | bytes 4194304 | tf_op jit(solution)/shard_map/reshape | solution.py:104
  213.9 4.1 %gather_fusion = bf16[128,4096]{1,0:T(8,128)(2,1)S(1)} fusion(bf16[256,4096]{1,0:T(8,128)(2,1)} %reshape.132, s32[1024]{0:T(1024)S(1)} %pad_clamp_fusion), kind=kCustom, calls=%fused_computation | custom fusion | bytes 2097664 | tf_op jit(solution)/shard_map/gather | solution.py:105
  218.0 0.8 fusion.16
  218.8 0.7 fusion.37
  (12 shorter events, 0.1 us)
Async XLA Ops:
  6.5 1.7 copy-start
  6.5 54.0 %all-gather.2.cloned.1.call-start = ((), (), s32[]{:S(2)}) async-start(), calls=%async_computation.4 | async-start | bytes 5242880 | tf_op jit(solution)/shard_map/all_gather | solution.py:61
  65.3 6.9 %copy-start.3 = (bf16[4096]{0:T(1024)(128)(2,1)S(1)}, bf16[4096]{0:T(1024)(128)(2,1)}, u32[]{:S(2)}) copy-start(bf16[4096]{0:T(1024)(128)(2,1)} %param.16) | copy-start | bytes 24580
  65.3 6.9 %copy-start.2 = (s32[16,8]{0,1:T(8,128)S(1)}, s32[16,8]{0,1:T(8,128)}, u32[]{:S(2)}) copy-start(s32[16,8]{0,1:T(8,128)} %param.21) | copy-start | bytes 1540
  65.3 34.8 %all-to-all-start.1 = ((bf16[16,16,4096]{2,1,0:T(8,128)(2,1)}), bf16[16,16,4096]{2,1,0:T(8,128)(2,1)}, u32[]{:S(2)}, u32[]{:S(2)}) async-start(bf16[16,16,4096]{2,1,0:T(8,128)(2,1)} %bitcast.67), calls=%async_computation.1 | async-start | bytes 4194304 | tf_op jit(solution)/shard_map/all_to_all | solution.py:63
  72.2 29.8 %copy-start.1 = (bf16[16,4096]{1,0:T(8,128)(2,1)S(1)}, bf16[16,4096]{1,0:T(8,128)(2,1)}, u32[]{:S(2)}) copy-start(bf16[16,4096]{1,0:T(8,128)(2,1)} %param.11) | copy-start | bytes 393220
  173.3 36.5 %all-to-all-start.3 = ((bf16[128,2,4096]{2,1,0:T(2,128)(2,1)}), bf16[128,2,4096]{2,1,0:T(2,128)(2,1)}, u32[]{:S(2)}, u32[]{:S(2)}) async-start(bf16[128,2,4096]{2,1,0:T(2,128)(2,1)} %reshape.131), calls=%async_computation.3 | async-start | bytes 4194304 | tf_op jit(solution)/shard_map/all_to_all | solution.py:103
Sparse Core Ops, SparseCore 0:
  9.0 51.4 all-gather.1

commit v2 on v0

v2 whole, which is shorter than its diff:
```python
import functools
import math

import jax
import jax.numpy as jnp
from jax import lax
from jax.experimental import pallas as pl
from jax.experimental.pallas import tpu as pltpu
from jax.sharding import PartitionSpec as P

MESH = pl.DeviceIdType.MESH
F32 = jnp.float32
BF16 = jnp.bfloat16

TOK = 16
D = 4096
HD = 128
KVH = 4
CTX = 128
HID = 768
EXPERTS = 128
STRIDE = (16, 4, 1)
START = (0, 1408, 2816)
WIDE = (1408, 1408, 1280)
ROT = tuple((r, (r + 1) % 3, (r + 2) % 3) for r in range(3))
ALL = 256


def iota(shape, dim):
    return lax.broadcasted_iota(jnp.int32, shape, dim)


def one_hot(mask):
    return jnp.where(mask, 1.0, 0.0).astype(BF16)


def dot(a, b):
    return jnp.dot(a, b, preferred_element_type=F32)


def dot_nt(a, b):
    return lax.dot_general(a, b, (((1,), (1,)), ((), ())), preferred_element_type=F32)


class Sems:
    def __init__(self, send, recv):
        self.send, self.recv, self.used = send, recv, 0

    def copy(self, src, dst, device):
        i = self.used
        self.used += 1
        return pltpu.make_async_remote_copy(
            src_ref=src,
            dst_ref=dst,
            send_sem=self.send.at[i],
            recv_sem=self.recv.at[i],
            device_id=device,
            device_id_type=MESH,
        )


N_COPIES = 9 + 9 + 45 + 18 + 36 + 42 + 18


def kernel(
    hidden_ref,
    query_ref,
    gain_ref,
    router_ref,
    routes_ref,
    key_hbm,
    value_hbm,
    ow_hbm,
    gate_hbm,
    up_hbm,
    down_hbm,
    out_ref,
    key_ref,
    value_ref,
    gate_ref,
    up_ref,
    down_ref,
    att,
    resid,
    normed,
    gate_acc,
    up_acc,
    *rest,
):
    rest = list(rest)

    def three():
        taken = rest[:3]
        del rest[:3]
        return taken

    weight, att_in, part1, over_b1, sum1, over_a1 = [three() for _ in range(6)]
    plane, plane_w, picked, rows, made, back = [three() for _ in range(6)]
    part2, over_b2, sum2, over_a2 = [three() for _ in range(4)]
    send, recv, local = rest
    sems = Sems(send, recv)

    pool = lax.axis_index("pool")
    dev = lax.axis_index("dev")
    at = (dev // 16, (dev // 4) % 4, dev % 4)

    def moved(*steps, other=0):
        where = list(at)
        for axis, step in steps:
            where[axis] = lax.rem(at[axis] + step, 4)
        there = where[0] * 16 + where[1] * 4 + where[2]
        return (lax.rem(pool + other, 2), there)

    def plus(axis, step):
        return lax.rem(at[axis] + step, 4)

    loads = []

    def load(src, dst):
        copy = pltpu.make_async_copy(src, dst, local.at[len(loads)])
        copy.start()
        loads.append(copy)
        return copy

    kv_loads = [load(key_hbm, key_ref), load(value_hbm, value_ref)]
    ow_loads = [
        load(ow_hbm.at[:, pl.ds(START[r], WIDE[r])], weight[r].at[at[ROT[r][0]]]) for r in range(3)
    ]
    expert_loads = [
        load(gate_hbm.at[0], gate_ref),
        load(up_hbm.at[0], up_ref),
        load(down_hbm.at[0], down_ref),
    ]

    barrier = pltpu.get_barrier_semaphore()
    partners = []
    for i in range(1, 64):
        steps = (i // 16, (i // 4) % 4, i % 4)
        moving = [(axis, step) for axis, step in enumerate(steps) if step]
        if len(moving) < 3:
            partners.append(moved(*moving))
    for axis in range(3):
        for step in range(1, 4):
            partners.append(moved((axis, step), other=1))
    partners.append(moved(other=1))
    for partner in partners:
        pl.semaphore_signal(barrier, inc=1, device_id=partner, device_id_type=MESH)
    pl.semaphore_wait(barrier, len(partners))

    half = pl.ds(pl.multiple_of(pool * 64, 64), 64)
    weight_out = []
    for r, (c, a, b) in enumerate(ROT):
        ow_loads[r].wait()
        mine = weight[r].at[at[c], half]
        for step in range(1, 4):
            copy = sems.copy(mine, mine, moved((c, step)))
            copy.start()
            weight_out.append(copy)

    for copy in kv_loads:
        copy.wait()
    row, col = iota((ALL, ALL), 0), iota((ALL, ALL), 1)
    swap = one_hot((row % TOK == col // TOK) & (row // TOK == col % TOK))
    for g in range(KVH):
        by_head = jnp.concatenate(
            [query_ref[:, pl.ds((g * TOK + h) * HD, HD)] for h in range(TOK)], axis=0
        )
        by_token = dot(swap, by_head).astype(BF16)
        lanes = pl.ds(g * HD, HD)
        scores = jnp.concatenate(
            [
                dot_nt(by_token[t * TOK : (t + 1) * TOK], key_ref[t, :, lanes])
                for t in range(TOK)
            ],
            axis=0,
        ) * (1.0 / math.sqrt(HD))
        top = jnp.max(scores, axis=-1, keepdims=True)
        raised = jnp.exp(scores - top)
        probs = (raised / jnp.sum(raised, axis=-1, keepdims=True)).astype(BF16)
        attended = jnp.concatenate(
            [dot(probs[t * TOK : (t + 1) * TOK], value_ref[t, :, lanes]) for t in range(TOK)],
            axis=0,
        ).astype(BF16)
        att[g] = dot(swap, attended).astype(BF16).reshape(4, 4, TOK, HD)

    att_out = []
    for r, (c, a, b) in enumerate(ROT):
        sent = []
        for step in range(16):
            step_b, step_a = step // 4, step % 4
            where = [None] * 3
            where[c] = pl.ds(0, 4)
            where[a], where[b] = plus(a, step_a), plus(b, step_b)
            src, dst = att.at[tuple(where)], att_in[r].at[at[b], at[a]]
            if step:
                copy = sems.copy(src, dst, moved((a, step_a), (b, step_b)))
                copy.start()
                sent.append(copy)
            else:
                own = pltpu.make_async_copy(src, dst, local.at[8 + r])
                own.start()
                sent.append(own)
        att_out.append(sent)

    twin_out = []
    for r, (c, a, b) in enumerate(ROT):
        for step in range(1, 4):
            weight_out[r * 3 + step - 1].wait_recv()
            held = weight[r].at[plus(c, 4 - step), half]
            copy = sems.copy(held, held, moved(other=1))
            copy.start()
            twin_out.append(copy)

    def scatter_b(r, part, over_b):
        c, a, b = ROT[r]
        sent = []
        for step in range(1, 4):
            copy = sems.copy(
                part[r].at[plus(b, step)], over_b[r].at[step - 1], moved((b, step))
            )
            copy.start()
            sent.append(copy)
        return sent

    def scatter_a(r, sent, part, over_b, summed, over_a):
        c, a, b = ROT[r]
        for copy in sent:
            copy.wait_recv()
        total = part[r][at[b]].astype(F32)
        for step in range(3):
            total = total + over_b[r][step].astype(F32)
        summed[r][...] = total.astype(BF16)
        out = []
        for step in range(1, 4):
            copy = sems.copy(
                summed[r].at[plus(a, step)], over_a[r].at[step - 1], moved((a, step))
            )
            copy.start()
            out.append(copy)
        return out

    def scattered(r, sent, summed, over_a):
        c, a, b = ROT[r]
        for copy in sent:
            copy.wait_recv()
        total = summed[r][at[a]].astype(F32)
        for step in range(3):
            total = total + over_a[r][step].astype(F32)
        return total

    b_out1 = []
    for r in range(3):
        for copy in twin_out[r * 3 : r * 3 + 3]:
            copy.wait_recv()
        for copy in att_out[r][1:]:
            copy.wait_recv()
        att_out[r][0].wait()
        held = att_in[r][...]
        lhs = jnp.concatenate(
            [held[:, :, c].reshape(ALL, HD) for c in range(4)], axis=1
        )
        rhs = weight[r][...].reshape(4 * HD, WIDE[r])
        part1[r][...] = dot(lhs, rhs).astype(BF16).reshape(4, 4, TOK, WIDE[r])
        b_out1.append(scatter_b(r, part1, over_b1))
    a_out1 = [scatter_a(r, b_out1[r], part1, over_b1, sum1, over_a1) for r in range(3)]
    square = jnp.zeros((TOK, 1), F32)
    for r in range(3):
        cols = pl.ds(START[r], WIDE[r])
        project = scattered(r, a_out1[r], sum1, over_a1)
        held = (hidden_ref[:, cols].astype(F32) + project).astype(BF16)
        resid[:, cols] = held
        held = held.astype(F32)
        square = square + jnp.sum(held * held, axis=-1, keepdims=True)
    scale = lax.rsqrt(square * (1.0 / D) + 1e-06)

    rows_a = []
    for r, (c, a, b) in enumerate(ROT):
        cols = pl.ds(START[r], WIDE[r])
        held = resid[:, cols].astype(F32) * scale * gain_ref[:, cols].astype(F32)
        held = held.astype(BF16)
        normed[:, cols] = held
        plane[r][at[b], at[a]] = held
        mine = plane[r].at[at[b], at[a]]
        sent = []
        for step in range(1, 4):
            copy = sems.copy(mine, mine, moved((a, step)))
            copy.start()
            sent.append(copy)
        rows_a.append(sent)

    logits = dot(normed[...], router_ref[...])
    ids = iota((TOK, EXPERTS), 1)
    routes = routes_ref[...]
    chosen = routes[:, 0:1] == ids
    for k in range(1, routes.shape[1]):
        chosen = chosen | (routes[:, k : k + 1] == ids)
    top = jnp.max(jnp.where(chosen, logits, -jnp.inf), axis=-1, keepdims=True)
    raised = jnp.where(chosen, jnp.exp(jnp.where(chosen, logits, top) - top), 0.0)
    shares = (raised / jnp.sum(raised, axis=-1, keepdims=True)).astype(BF16)
    shares_a = []
    for r, (c, a, b) in enumerate(ROT):
        plane_w[r][at[b], at[a]] = shares
        mine = plane_w[r].at[at[b], at[a]]
        sent = []
        for step in range(1, 4):
            copy = sems.copy(mine, mine, moved((a, step)))
            copy.start()
            sent.append(copy)
        shares_a.append(sent)

    rows_b, shares_b = [], []
    for r, (c, a, b) in enumerate(ROT):
        for held, before, after in (
            (plane_w[r], shares_a[r], shares_b),
            (plane[r], rows_a[r], rows_b),
        ):
            for copy in before:
                copy.wait_recv()
            sent = []
            for step in range(1, 4):
                copy = sems.copy(held.at[at[b]], held.at[at[b]], moved((b, step)))
                copy.start()
                sent.append(copy)
            after.append(sent)

    same = row // TOK == col // TOK
    line_out, combine = [], []
    for r, (c, a, b) in enumerate(ROT):
        for copy in shares_b[r]:
            copy.wait_recv()
        own = at[a] * STRIDE[a] + at[b] * STRIDE[b]

        def expert(slot):
            return slot // 64 * STRIDE[c] + slot // 32 % 2 * 64 + own

        held = plane_w[r][...].reshape(ALL, EXPERTS)
        names = one_hot(expert(iota((ALL, EXPERTS), 0)) == iota((ALL, EXPERTS), 1))
        share = dot_nt(names, held)
        uses = share > 0
        rank = dot(one_hot(uses), one_hot(same & (row < col)))
        uses = uses & (rank == (row % 2).astype(F32)) & (row // 2 % 16 == col // TOK)
        select = one_hot(uses)
        share = dot_nt(held, names)
        uses = share > 0
        rank = dot(one_hot(same & (col < row)), one_hot(uses))
        uses = uses & (rank == (col % 2).astype(F32)) & (col // 2 % 16 == row // TOK)
        combine.append(jnp.where(uses, share, 0.0).astype(BF16))
        for copy in rows_b[r]:
            copy.wait_recv()
        outgoing = dot(select, plane[r][...].reshape(ALL, WIDE[r])).astype(BF16)
        picked[r][...] = outgoing.reshape(4, 2, 32, WIDE[r])
        sent = []
        for step in range(1, 8):
            step_p, step_c = step // 4, step % 4
            copy = sems.copy(
                picked[r].at[plus(c, step_c), lax.rem(pool + step_p, 2)],
                rows[r].at[at[c], pool],
                moved((c, step_c), other=step_p),
            )
            copy.start()
            sent.append(copy)
        rows[r][at[c], pool] = picked[r][at[c], pool]
        line_out.append(sent)

    for copy in expert_loads:
        copy.wait()

    def place(slot, r):
        rank = slot % 2
        coord = {0: slot // 64, 2: slot // 8 % 4, 1: slot // 2 % 4}
        core = slot // 32 % 2
        c, a, b = ROT[r]
        return coord[c] * 64 + core * 32 + coord[b] * 8 + coord[a] * 2 + rank

    for r in range(3):
        for copy in line_out[r]:
            copy.wait_recv()
        held = rows[r][...].reshape(ALL, WIDE[r])
        if r:
            held = dot(one_hot(place(row, r) == col), held).astype(BF16)
        cols = pl.ds(START[r], WIDE[r])
        gate = dot(held, gate_ref[cols, :])
        up = dot(held, up_ref[cols, :])
        if r:
            gate, up = gate_acc[...] + gate, up_acc[...] + up
        gate_acc[...] = gate
        up_acc[...] = up
    gate = gate_acc[...]
    activated = (gate / (1.0 + jnp.exp(-gate)) * up_acc[...]).astype(BF16)
    line_back = []
    for r, (c, a, b) in enumerate(ROT):
        held = activated
        if r:
            held = dot(one_hot(place(col, r) == row), held).astype(BF16)
        result = dot(held, down_ref[:, pl.ds(START[r], WIDE[r])]).astype(BF16)
        made[r][...] = result.reshape(4, 2, 32, WIDE[r])
        sent = []
        for step in range(1, 8):
            step_p, step_c = step // 4, step % 4
            copy = sems.copy(
                made[r].at[plus(c, step_c), lax.rem(pool + step_p, 2)],
                back[r].at[at[c], pool],
                moved((c, step_c), other=step_p),
            )
            copy.start()
            sent.append(copy)
        back[r][at[c], pool] = made[r][at[c], pool]
        line_back.append(sent)

    b_out2 = []
    for r in range(3):
        for copy in line_back[r]:
            copy.wait_recv()
        total = dot(combine[r], back[r][...].reshape(ALL, WIDE[r]))
        part2[r][...] = total.astype(BF16).reshape(4, 4, TOK, WIDE[r])
        b_out2.append(scatter_b(r, part2, over_b2))
    a_out2 = [scatter_a(r, b_out2[r], part2, over_b2, sum2, over_a2) for r in range(3)]
    for r in range(3):
        cols = pl.ds(START[r], WIDE[r])
        mixture = scattered(r, a_out2[r], sum2, over_a2)
        out_ref[:, cols] = (resid[:, cols].astype(F32) + mixture).astype(BF16)

    sent = weight_out + twin_out
    for group in (b_out1, a_out1, rows_a, shares_a, rows_b, shares_b, line_out, line_back, b_out2, a_out2):
        for copies in group:
            sent += copies
    for copies in att_out:
        sent += copies[1:]
    for copy in sent:
        copy.wait_send()


def shards(hidden, queries, k_cache, v_cache, o_weight, norm_gain, router_weight, w_gate, w_up, w_down, routes):
    vmem, hbm = pl.BlockSpec(memory_space=pltpu.VMEM), pl.BlockSpec(memory_space=pl.ANY)

    def three(*lead, cols=None):
        return [pltpu.VMEM((*lead, cols or wide), BF16) for wide in WIDE]

    scratch = [
        pltpu.VMEM((TOK, CTX, KVH * HD), BF16),
        pltpu.VMEM((TOK, CTX, KVH * HD), BF16),
        pltpu.VMEM((D, HID), BF16),
        pltpu.VMEM((D, HID), BF16),
        pltpu.VMEM((HID, D), BF16),
        pltpu.VMEM((4, 4, 4, TOK, HD), BF16),
        pltpu.VMEM((TOK, D), BF16),
        pltpu.VMEM((TOK, D), BF16),
        pltpu.VMEM((ALL, HID), F32),
        pltpu.VMEM((ALL, HID), F32),
        *three(4, HD),
        *three(4, 4, 4, TOK, cols=HD),
        *three(4, 4, TOK),
        *three(3, 4, TOK),
        *three(4, TOK),
        *three(3, TOK),
        *three(4, 4, TOK),
        *three(4, 4, TOK, cols=EXPERTS),
        *three(4, 2, 32),
        *three(4, 2, 32),
        *three(4, 2, 32),
        *three(4, 2, 32),
        *three(4, 4, TOK),
        *three(3, 4, TOK),
        *three(4, TOK),
        *three(3, TOK),
        pltpu.SemaphoreType.DMA((N_COPIES,)),
        pltpu.SemaphoreType.DMA((N_COPIES,)),
        pltpu.SemaphoreType.DMA((11,)),
    ]
    return pl.pallas_call(
        kernel,
        out_shape=jax.ShapeDtypeStruct((TOK, D), BF16),
        in_specs=[vmem] * 5 + [hbm] * 6,
        out_specs=vmem,
        scratch_shapes=scratch,
        compiler_params=pltpu.CompilerParams(
            collective_id=0, has_side_effects=True, vmem_limit_bytes=60 * 1024 * 1024
        ),
    )(
        hidden,
        queries,
        norm_gain.reshape(1, D),
        router_weight,
        routes,
        k_cache,
        v_cache,
        o_weight,
        w_gate,
        w_up,
        w_down,
    )


def solution(mesh):
    rows = P(("pool", "dev"), None)
    cube = P(("pool", "dev"), None, None)
    placed = (rows, rows, cube, cube, P("dev", None), P(), P(), cube, cube, cube, rows)
    return jax.shard_map(shards, mesh=mesh, in_specs=placed, out_specs=rows, check_vma=False)
```

time: 553 us -> 103 us (0.19)
  waiting for transfers between devices: 362 us -> 0 us
  blocking collectives: 107 us -> 0 us
  Pallas kernels: 0 us -> 97.7 us
  matrix products: 34.9 us -> 0 us
  local copies, waits for them, and re-layouts: 25.6 us -> 4.23 us
  between operations: 13.5 us -> 0.01 us
  starting transfers between devices: 6.31 us -> 0 us
    reduce_scatter x1 -> x0, waiting for transfers between devices: 335 us -> none  [shards(): lax.psum_scatter(jnp.dot(head_rows, o_weight, preferred_element_type=jnp....]
    all_to_all x2 -> x0, blocking collectives: 107 us -> none  [the longest x1 85.9 us: shards(): lax.all_to_all(outgoing, ('pool', 'dev'), split_axis=0, concat_axis=0, ti...]
    pallas_call x0 -> x1, Pallas kernels: none -> 97.7 us  [shards(): pl.pallas_call(kernel, out_shape=jax.ShapeDtypeStruct((TOK, D), BF16), in...]
    dot_general x7 -> x0, matrix products: 34.9 us -> none  [the longest x1 11.3 us: expert_rows(): jnp.dot(activated, down_weight, preferred_element_type=jnp.float32)]
    all_to_all x1 -> x0, waiting for transfers between devices: 26.8 us -> none  [shards(): lax.all_to_all(produced, ('pool', 'dev'), split_axis=0, concat_axis=0, ti...]
    reshape x5 -> x1, local copies, waits for them, and re-layouts: 17.2 us -> 1.31 us  [shards(): norm_gain.reshape(1, D)]
    all_to_all x1 -> x0, starting transfers between devices: 6.31 us -> none  [shards(): lax.all_to_all(produced, ('pool', 'dev'), split_axis=0, concat_axis=0, ti...]
    gather x6 -> x0, local copies, waits for them, and re-layouts: 5.63 us -> none  [the longest x1 4.06 us: shards(): returned[position].astype(jnp.float32).reshape(tok_rows, -1, model_width)]
  transfers between devices with their start and end apart: 2 -> 0, of which waited for: 2 -> 0; matrix products, arithmetic and copies ran while one was open for 1% -> 0% of each run, Pallas kernels for 0% -> 0%
where the time goes in v2:
time: 103 us; the launch traced here: 102 us
  Pallas kernels  97.7 us (95%)
  local copies, waits for them, and re-layouts  4.23 us (4%)
    pallas_call x1, Pallas kernels, shards(): pl.pallas_call(kernel, out_shape=jax.ShapeDtypeStruct((TOK, D), BF16), in...  97.7 us
    unnamed x2, local copies, waits for them, and re-layouts  2.92 us

profile of v2, /device:TPU:1, one launch (start us, length us, event | category | flops | bytes accessed | tf_op | source)
XLA Modules:
  0.0 102.0 jit_solution(14653860775830443311)
XLA Ops:
  0.0 1.4 %copy.12.routes_ref = s32[16,8]{1,0:T(8,128)} copy(s32[16,8]{0,1:T(8,128)} %param.21) | data formatting | bytes 1024 | tf_op args[10]
  1.4 1.3 %reshape.3.gain_ref = bf16[1,4096]{1,0:T(2,128)(2,1)} reshape(bf16[4096]{0:T(1024)(128)(2,1)} %param.16) | data formatting | bytes 16384 | tf_op jit(solution)/shard_map/reshape | solution.py:482
  2.7 97.7 %shard_map.109 = bf16[16,4096]{1,0:T(8,128)(2,1)} custom-call(bf16[16,4096]{1,0:T(8,128)(2,1)} %hidden_ref.1, bf16[16,8192]{1,0:T(8,128)(2,1)} %query_ref.1, bf16[1,4096]{1,0:T(2,128)(2,1)} %reshape.3.gain_ref, bf16[4096,128]{1,0:T(8,128)(2,1)} %router_ref.1, s32[16,8]{1,0:T(8,128)} %copy.12.routes_ref, bf16[16,128,512]{2,1,0:T(8,128)(2,1)} %key_hbm.1, ...), custom_call_target="tpu_custom_call" | custom-call | tf_op jit(solution)/shard_map/pallas_call | solution.py:470
  100.4 1.6 %copy.14 = bf16[16,4096]{1,0:T(8,128)(2,1)} copy(bf16[16,4096]{1,0:T(8,128)(2,1)} %shard_map.109) | data formatting | bytes 262144

commit v3 on v0

v3 whole, which is shorter than its diff:
```python
import functools
import math

import jax
import jax.numpy as jnp
from jax import lax
from jax.experimental import pallas as pl
from jax.experimental.pallas import tpu as pltpu
from jax.sharding import PartitionSpec as P

MESH = pl.DeviceIdType.MESH
F32 = jnp.float32
BF16 = jnp.bfloat16

TOK = 16
D = 4096
HD = 128
KVH = 4
CTX = 128
HID = 768
EXPERTS = 128
STRIDE = (16, 4, 1)
START = (0, 512, 1024, 1536, 2048, 2560, 2944, 3328, 3712)
WIDE = (512, 512, 512, 512, 512, 384, 384, 384, 384)
PARTS = len(WIDE)
ROT = tuple((p % 3, (p + 1) % 3, (p + 2) % 3) for p in range(PARTS))
NEAR_FIRST = (1, 3, 2)
ALL = 256


def iota(shape, dim):
    return lax.broadcasted_iota(jnp.int32, shape, dim)


def one_hot(mask):
    return jnp.where(mask, 1.0, 0.0).astype(BF16)


def dot(a, b):
    return jnp.dot(a, b, preferred_element_type=F32)


def dot_nt(a, b):
    return lax.dot_general(a, b, (((1,), (1,)), ((), ())), preferred_element_type=F32)


class Group:
    def __init__(self, sems, like):
        self.send, self.recv = sems
        self.like = like

    def push(self, src, dst, device):
        pltpu.make_async_remote_copy(
            src_ref=src,
            dst_ref=dst,
            send_sem=self.send,
            recv_sem=self.recv,
            device_id=device,
            device_id_type=MESH,
        ).start()

    def arrived(self):
        pltpu.make_async_copy(self.like, self.like, self.recv).wait()

    def sent(self):
        pltpu.make_async_copy(self.like, self.like, self.send).wait()


N_GROUPS = 11 * PARTS + 11
N_LOADS = 9


def kernel(
    gain_ref,
    routes_ref,
    hidden_hbm,
    query_hbm,
    router_hbm,
    key_hbm,
    value_hbm,
    ow_hbm,
    gate_hbm,
    up_hbm,
    down_hbm,
    out_ref,
    hidden_ref,
    query_ref,
    router_ref,
    key_ref,
    value_ref,
    gate_ref,
    up_ref,
    down_ref,
    ow_ref,
    att,
    mid_x,
    mid_z,
    resid,
    normed,
    gate_acc,
    up_acc,
    *rest,
):
    rest = list(rest)

    def take(count):
        taken = rest[:count]
        del rest[:count]
        return taken

    att_in, plane_w = take(3), take(3)
    weight, part1, over_b1, sum1, over_a1 = [take(PARTS) for _ in range(5)]
    plane, picked, rows, made, back = [take(PARTS) for _ in range(5)]
    part2, over_b2, sum2, over_a2 = [take(PARTS) for _ in range(4)]
    send, recv, local = rest
    groups = []

    def group(like):
        i = len(groups)
        groups.append(Group((send.at[i], recv.at[i]), like))
        return groups[i]


    pool = lax.axis_index("pool")
    dev = lax.axis_index("dev")
    at = (dev // 16, (dev // 4) % 4, dev % 4)

    def moved(*steps, other=0):
        where = list(at)
        for axis, step in steps:
            where[axis] = lax.rem(at[axis] + step, 4)
        there = where[0] * 16 + where[1] * 4 + where[2]
        return (lax.rem(pool + other, 2), there)

    def plus(axis, step):
        return lax.rem(at[axis] + step, 4)

    def drain(*copies):
        for copy in copies:
            copy.sent()

    barrier = pltpu.get_barrier_semaphore()
    partners = [moved(other=1)]
    for axis in range(3):
        for step in range(1, 4):
            partners += [moved((axis, step)), moved((axis, step), other=1)]
    for partner in partners:
        pl.semaphore_signal(barrier, inc=1, device_id=partner, device_id_type=MESH)

    loads = []

    def load(src, dst):
        copy = pltpu.make_async_copy(src, dst, local.at[len(loads)])
        copy.start()
        loads.append(copy)
        return copy

    ow_load, query_load, key_load, value_load = [
        load(src, dst)
        for src, dst in (
            (ow_hbm, ow_ref),
            (query_hbm, query_ref),
            (key_hbm, key_ref),
            (value_hbm, value_ref),
        )
    ]

    row, col = iota((ALL, ALL), 0), iota((ALL, ALL), 1)
    swap = one_hot((row % TOK == col // TOK) & (row // TOK == col % TOK))

    def attend():
        empty = jnp.zeros((TOK, HD), BF16)
        asked = []
        for g in range(KVH):
            by_head = jnp.concatenate(
                [query_ref[:, (g * TOK + h) * HD : (g * TOK + h + 1) * HD] for h in range(TOK)],
                axis=0,
            )
            asked.append(dot(swap, by_head).astype(BF16))
        scores = []
        for t in range(TOK):
            rows = [
                jnp.concatenate(
                    [asked[g][t * TOK : (t + 1) * TOK] if g == i else empty for i in range(KVH)],
                    axis=1,
                )
                for g in range(KVH)
            ]
            scores.append(dot_nt(jnp.concatenate(rows, axis=0), key_ref[t]))
        scores = jnp.concatenate(scores, axis=0) * (1.0 / math.sqrt(HD))
        top = jnp.max(scores, axis=-1, keepdims=True)
        raised = jnp.exp(scores - top)
        probs = (raised / jnp.sum(raised, axis=-1, keepdims=True)).astype(BF16)
        wide = KVH * TOK
        found = [dot(probs[t * wide : (t + 1) * wide], value_ref[t]) for t in range(TOK)]
        for g in range(KVH):
            rows, lanes = slice(g * TOK, (g + 1) * TOK), slice(g * HD, (g + 1) * HD)
            attended = jnp.concatenate([held[rows, lanes] for held in found], axis=0)
            att[g] = dot(swap, attended.astype(BF16)).astype(BF16).reshape(4, 4, TOK, HD)

    half = pl.ds(pl.multiple_of(pool * 64, 64), 64)
    quarters = [pl.ds(pl.multiple_of(pool * 64 + i, 32), 32) for i in (0, 32)]
    weight_near, weight_far, twin = [], [], []

    def send_weight(p):
        c, a, b = ROT[p]
        cols = pl.ds(START[p], WIDE[p])
        src, dst = ow_ref.at[half, cols], weight[p].at[at[c], half]
        copies = group(weight[p].at[0])
        for hop in (1, 3):
            copies.push(src, dst, moved((c, hop)))
        weight_near.append(copies)
        weight[p][at[c]] = ow_ref[:, cols]

    def pass_weight(p):
        c, a, b = ROT[p]
        weight_near[p].arrived()
        copies = group(weight[p].at[0, 0:64])
        for hop, rows in ((1, quarters[0]), (3, quarters[1])):
            held = weight[p].at[plus(c, 4 - hop), rows]
            copies.push(held, held, moved((c, hop)))
        weight_far.append(copies)
        copies = group(weight[p].at[0:3, 0:64])
        for hop in (1, 3):
            held = weight[p].at[plus(c, hop), half]
            copies.push(held, held, moved(other=1))
        twin.append(copies)

    def hand_over(p):
        c, a, b = ROT[p]
        weight_far[p].arrived()
        held = weight[p].at[plus(c, 2), half]
        twin[p].push(held, held, moved(other=1))

    query_load.wait()
    key_load.wait()
    value_load.wait()
    attend()
    pl.semaphore_wait(barrier, len(partners))
    over_x, over_z = group(mid_x.at[0:3]), group(mid_z.at[0:3])
    for hop in NEAR_FIRST:
        over_x.push(att.at[plus(0, hop)], mid_x.at[at[0]], moved((0, hop)))
        over_z.push(att.at[:, plus(1, hop)], mid_z.at[at[1]], moved((1, hop)))
    ow_load.wait()
    for p in range(PARTS):
        send_weight(p)
    mid_x[at[0]] = att[at[0]]
    mid_z[at[1]] = att[:, at[1]]
    att_out = [group(att_in[r].at[0:3]) for r in range(3)]
    over_x.arrived()
    for hop in NEAR_FIRST:
        att_out[2].push(mid_x.at[:, plus(1, hop)], att_in[2].at[at[1]], moved((1, hop)))
        att_out[1].push(mid_x.at[:, :, plus(2, hop)], att_in[1].at[:, at[2]], moved((2, hop)))
    over_z.arrived()
    for hop in NEAR_FIRST:
        att_out[0].push(mid_z.at[:, :, plus(2, hop)], att_in[0].at[at[2]], moved((2, hop)))
    att_in[2][at[1]] = mid_x[:, at[1]]
    att_in[1][:, at[2]] = mid_x[:, :, at[2]]
    att_in[0][at[2]] = mid_z[:, :, at[2]]
    for p in range(PARTS):
        pass_weight(p)
    for p in range(PARTS):
        hand_over(p)
    small_loads = [load(hidden_hbm, hidden_ref), load(router_hbm, router_ref)]
    expert_loads = [
        load(gate_hbm.at[0], gate_ref),
        load(up_hbm.at[0], up_ref),
        load(down_hbm.at[0], down_ref),
    ]

    def scatter_b(p, part, over_b):
        c, a, b = ROT[p]
        copies = group(over_b[p])
        for hop in NEAR_FIRST:
            copies.push(part[p].at[plus(b, hop)], over_b[p].at[hop - 1], moved((b, hop)))
        return copies

    def scatter_a(p, before, part, over_b, summed, over_a):
        c, a, b = ROT[p]
        before.arrived()
        total = part[p][at[b]].astype(F32)
        for i in range(3):
            total = total + over_b[p][i].astype(F32)
        summed[p][...] = total.astype(BF16)
        copies = group(over_a[p])
        for hop in NEAR_FIRST:
            copies.push(summed[p].at[plus(a, hop)], over_a[p].at[hop - 1], moved((a, hop)))
        return copies

    def scattered(p, copies, summed, over_a):
        c, a, b = ROT[p]
        copies.arrived()
        total = summed[p][at[a]].astype(F32)
        for i in range(3):
            total = total + over_a[p][i].astype(F32)
        return total

    b_out1 = []
    lhs = []
    for p in range(PARTS):
        if p < 3:
            att_out[p].arrived()
            held = att_in[p][...]
            lhs.append(
                jnp.concatenate([held[:, :, i].reshape(ALL, HD) for i in range(4)], axis=1)
            )
        twin[p].arrived()
        rhs = weight[p][...].reshape(4 * HD, WIDE[p])
        part1[p][...] = dot(lhs[p % 3], rhs).astype(BF16).reshape(4, 4, TOK, WIDE[p])
        b_out1.append(scatter_b(p, part1, over_b1))
    drain(over_x, over_z, *weight_near, *weight_far, *twin)

    squares = []
    rows_a = []
    a_out1 = [scatter_a(p, b_out1[p], part1, over_b1, sum1, over_a1) for p in range(PARTS)]

    def finish(p):
        c, a, b = ROT[p]
        cols = pl.ds(START[p], WIDE[p])
        held = (hidden_ref[:, cols].astype(F32) + scattered(p, a_out1[p], sum1, over_a1)).astype(
            BF16
        )
        resid[:, cols] = held
        plane[p][at[b], at[a]] = held
        mine = plane[p].at[at[b], at[a]]
        copies = group(plane[p].at[0, 0:3])
        for hop in NEAR_FIRST:
            copies.push(mine, mine, moved((a, hop)))
        rows_a.append(copies)
        held = held.astype(F32)
        squares.append(jnp.sum(held * held, axis=-1, keepdims=True))

    def gather_b(p):
        c, a, b = ROT[p]
        rows_a[p].arrived()
        mine = plane[p].at[at[b]]
        copies = group(plane[p].at[0:3])
        for hop in NEAR_FIRST:
            copies.push(mine, mine, moved((b, hop)))
        return copies

    for copy in small_loads:
        copy.wait()
    for p in range(PARTS):
        finish(p)
    rows_b = [gather_b(p) for p in range(3)]
    scale = lax.rsqrt(sum(squares) * (1.0 / D) + 1e-06)

    def norm(held, scale, i):
        held = held.astype(F32) * scale * gain_ref[i // 128 : i // 128 + 1, :].astype(F32)
        return held.astype(BF16)

    for i in range(0, D, 128):
        normed[:, i : i + 128] = norm(resid[:, i : i + 128], scale, i)

    logits = dot(normed[...], router_ref[...])
    ids = iota((TOK, EXPERTS), 1)
    eye = one_hot(iota((TOK, TOK), 0) == iota((TOK, TOK), 1))
    routes = dot_nt(eye, routes_ref[...].astype(F32).astype(BF16)).astype(jnp.int32)
    chosen = routes[:, 0:1] == ids
    for k in range(1, routes.shape[1]):
        chosen = chosen | (routes[:, k : k + 1] == ids)
    top = jnp.max(jnp.where(chosen, logits, -jnp.inf), axis=-1, keepdims=True)
    raised = jnp.where(chosen, jnp.exp(jnp.where(chosen, logits, top) - top), 0.0)
    shares = (raised / jnp.sum(raised, axis=-1, keepdims=True)).astype(BF16)
    lane = iota((TOK, EXPERTS), 1)
    high = scale.astype(BF16).astype(F32)
    middle = (scale - high).astype(BF16).astype(F32)
    low = scale - high - middle
    scales = jnp.where(lane == 0, high, jnp.where(lane == 1, middle, jnp.where(lane == 2, low, 0.0)))
    shares_a = []
    for r in range(3):
        c, a, b = ROT[r]
        plane_w[r][at[b], at[a], :, 0:EXPERTS] = shares
        plane_w[r][at[b], at[a], :, EXPERTS : 2 * EXPERTS] = scales.astype(BF16)
        mine = plane_w[r].at[at[b], at[a]]
        copies = group(plane_w[r].at[0, 0:3])
        for hop in NEAR_FIRST:
            copies.push(mine, mine, moved((a, hop)))
        shares_a.append(copies)

    rows_b += [gather_b(p) for p in range(3, PARTS)]
    shares_b = []
    for r in range(3):
        c, a, b = ROT[r]
        shares_a[r].arrived()
        mine = plane_w[r].at[at[b]]
        copies = group(plane_w[r].at[0:3])
        for hop in NEAR_FIRST:
            copies.push(mine, mine, moved((b, hop)))
        shares_b.append(copies)
    drain(*att_out, *b_out1, *a_out1, *rows_a, *shares_a)

    same = row // TOK == col // TOK
    select, combine, scales = [], [], []
    for r in range(3):
        c, a, b = ROT[r]
        shares_b[r].arrived()
        own = at[a] * STRIDE[a] + at[b] * STRIDE[b]

        def expert(slot):
            return slot // 64 * STRIDE[c] + slot // 32 % 2 * 64 + own

        held = plane_w[r][...].reshape(ALL, 2 * EXPERTS)
        scales.append(jnp.sum(held[:, EXPERTS:].astype(F32), axis=-1, keepdims=True))
        held = held[:, :EXPERTS]
        names = one_hot(expert(iota((ALL, EXPERTS), 0)) == iota((ALL, EXPERTS), 1))
        share = dot_nt(names, held)
        uses = share > 0
        rank = dot(one_hot(uses), one_hot(same & (row < col)))
        uses = uses & (rank == (row % 2).astype(F32)) & (row // 2 % 16 == col // TOK)
        select.append(one_hot(uses))
        share = dot_nt(held, names)
        uses = share > 0
        rank = dot(one_hot(same & (col < row)), one_hot(uses))
        uses = uses & (rank == (col % 2).astype(F32)) & (col // 2 % 16 == row // TOK)
        combine.append(jnp.where(uses, share, 0.0).astype(BF16))

    def along_line(p, src, dst):
        c, a, b = ROT[p]
        copies = group(src[p].at[0:7])
        for step in (1, 3, 5, 7, 2, 6, 4):
            step_p, step_c = step // 4, step % 4
            there = plus(c, step_c) * 2 + lax.rem(pool + step_p, 2)
            copies.push(
                src[p].at[there], dst[p].at[at[c] * 2 + pool], moved((c, step_c), other=step_p)
            )
        dst[p][at[c] * 2 + pool] = src[p][at[c] * 2 + pool]
        return copies

    line_out = []
    for p in range(PARTS):
        rows_b[p].arrived()
        held = plane[p][...].reshape(ALL, WIDE[p])
        held = jnp.concatenate(
            [
                norm(held[:, i : i + 128], scales[p % 3], START[p] + i)
                for i in range(0, WIDE[p], 128)
            ],
            axis=1,
        )
        outgoing = dot(select[p % 3], held).astype(BF16)
        picked[p][...] = outgoing.reshape(8, 32, WIDE[p])
        line_out.append(along_line(p, picked, rows))
    drain(*rows_b, *shares_b)

    for copy in expert_loads:
        copy.wait()

    def place(slot, r):
        rank = slot % 2
        coord = {0: slot // 64, 2: slot // 8 % 4, 1: slot // 2 % 4}
        core = slot // 32 % 2
        c, a, b = ROT[r]
        return coord[c] * 64 + core * 32 + coord[b] * 8 + coord[a] * 2 + rank

    for p in range(PARTS):
        line_out[p].arrived()
        held = rows[p][...].reshape(ALL, WIDE[p])
        if p % 3:
            held = dot(one_hot(place(row, p % 3) == col), held).astype(BF16)
        cols = pl.ds(START[p], WIDE[p])
        gate = dot(held, gate_ref[cols, :])
        up = dot(held, up_ref[cols, :])
        if p:
            gate, up = gate_acc[...] + gate, up_acc[...] + up
        gate_acc[...] = gate
        up_acc[...] = up
    gate = gate_acc[...]
    activated = (gate / (1.0 + jnp.exp(-gate)) * up_acc[...]).astype(BF16)
    activated = [activated] + [
        dot(one_hot(place(col, r) == row), activated).astype(BF16) for r in (1, 2)
    ]
    line_back = []
    for p in range(PARTS):
        result = dot(activated[p % 3], down_ref[:, pl.ds(START[p], WIDE[p])]).astype(BF16)
        made[p][...] = result.reshape(8, 32, WIDE[p])
        line_back.append(along_line(p, made, back))
    drain(*line_out)

    b_out2 = []
    for p in range(PARTS):
        line_back[p].arrived()
        total = dot(combine[p % 3], back[p][...].reshape(ALL, WIDE[p]))
        part2[p][...] = total.astype(BF16).reshape(4, 4, TOK, WIDE[p])
        b_out2.append(scatter_b(p, part2, over_b2))
    drain(*line_back)
    a_out2 = [scatter_a(p, b_out2[p], part2, over_b2, sum2, over_a2) for p in range(PARTS)]
    drain(*b_out2)
    for p in range(PARTS):
        cols = pl.ds(START[p], WIDE[p])
        mixture = scattered(p, a_out2[p], sum2, over_a2)
        out_ref[:, cols] = (resid[:, cols].astype(F32) + mixture).astype(BF16)
    drain(*a_out2)


def shards(hidden, queries, k_cache, v_cache, o_weight, norm_gain, router_weight, w_gate, w_up, w_down, routes):
    vmem, hbm = pl.BlockSpec(memory_space=pltpu.VMEM), pl.BlockSpec(memory_space=pl.ANY)

    def parts(*lead):
        return [pltpu.VMEM((*lead, wide), BF16) for wide in WIDE]

    scratch = [
        pltpu.VMEM((TOK, D), BF16),
        pltpu.VMEM((TOK, 2 * D), BF16),
        pltpu.VMEM((D, EXPERTS), BF16),
        pltpu.VMEM((TOK, CTX, KVH * HD), BF16),
        pltpu.VMEM((TOK, CTX, KVH * HD), BF16),
        pltpu.VMEM((D, HID), BF16),
        pltpu.VMEM((D, HID), BF16),
        pltpu.VMEM((HID, D), BF16),
        pltpu.VMEM((HD, D), BF16),
        *[pltpu.VMEM((4, 4, 4, TOK, HD), BF16)] * 3,
        pltpu.VMEM((TOK, D), BF16),
        pltpu.VMEM((TOK, D), BF16),
        pltpu.VMEM((ALL, HID), F32),
        pltpu.VMEM((ALL, HID), F32),
        *[pltpu.VMEM((4, 4, 4, TOK, HD), BF16)] * 3,
        *[pltpu.VMEM((4, 4, TOK, 2 * EXPERTS), BF16)] * 3,
        *parts(4, HD),
        *parts(4, 4, TOK),
        *parts(3, 4, TOK),
        *parts(4, TOK),
        *parts(3, TOK),
        *parts(4, 4, TOK),
        *parts(8, 32),
        *parts(8, 32),
        *parts(8, 32),
        *parts(8, 32),
        *parts(4, 4, TOK),
        *parts(3, 4, TOK),
        *parts(4, TOK),
        *parts(3, TOK),
        pltpu.SemaphoreType.DMA((N_GROUPS,)),
        pltpu.SemaphoreType.DMA((N_GROUPS,)),
        pltpu.SemaphoreType.DMA((N_LOADS,)),
    ]
    return pl.pallas_call(
        kernel,
        out_shape=jax.ShapeDtypeStruct((TOK, D), BF16),
        in_specs=[vmem] * 2 + [hbm] * 9,
        out_specs=vmem,
        scratch_shapes=scratch,
        compiler_params=pltpu.CompilerParams(
            collective_id=0, has_side_effects=True, vmem_limit_bytes=60 * 1024 * 1024
        ),
    )(
        norm_gain.reshape(D // 128, 128),
        routes.T,
        hidden,
        queries,
        router_weight,
        k_cache,
        v_cache,
        o_weight,
        w_gate,
        w_up,
        w_down,
    )


def solution(mesh):
    rows = P(("pool", "dev"), None)
    cube = P(("pool", "dev"), None, None)
    placed = (rows, rows, cube, cube, P("dev", None), P(), P(), cube, cube, cube, rows)
    return jax.shard_map(shards, mesh=mesh, in_specs=placed, out_specs=rows, check_vma=False)
```

time: 553 us -> 90.8 us (0.16)
  waiting for transfers between devices: 362 us -> 0 us
  blocking collectives: 107 us -> 0 us
  Pallas kernels: 0 us -> 89.1 us
  matrix products: 34.9 us -> 0 us
  local copies, waits for them, and re-layouts: 25.6 us -> 1.57 us
  between operations: 13.5 us -> 0.01 us
  starting transfers between devices: 6.31 us -> 0 us
    reduce_scatter x1 -> x0, waiting for transfers between devices: 335 us -> none  [shards(): lax.psum_scatter(jnp.dot(head_rows, o_weight, preferred_element_type=jnp....]
    all_to_all x2 -> x0, blocking collectives: 107 us -> none  [the longest x1 85.9 us: shards(): lax.all_to_all(outgoing, ('pool', 'dev'), split_axis=0, concat_axis=0, ti...]
    pallas_call x0 -> x1, Pallas kernels: none -> 89.1 us  [shards(): pl.pallas_call(kernel, out_shape=jax.ShapeDtypeStruct((TOK, D), BF16), in...]
    dot_general x7 -> x0, matrix products: 34.9 us -> none  [the longest x1 11.3 us: expert_rows(): jnp.dot(activated, down_weight, preferred_element_type=jnp.float32)]
    all_to_all x1 -> x0, waiting for transfers between devices: 26.8 us -> none  [shards(): lax.all_to_all(produced, ('pool', 'dev'), split_axis=0, concat_axis=0, ti...]
    reshape x5 -> x0, local copies, waits for them, and re-layouts: 17.2 us -> none  [the longest x1 4.4 us: expert_block(): expert_rows(flat_rows, gate_weight, up_weight, down_weight)]
    all_to_all x1 -> x0, starting transfers between devices: 6.31 us -> none  [shards(): lax.all_to_all(produced, ('pool', 'dev'), split_axis=0, concat_axis=0, ti...]
    gather x6 -> x0, local copies, waits for them, and re-layouts: 5.63 us -> none  [the longest x1 4.06 us: shards(): returned[position].astype(jnp.float32).reshape(tok_rows, -1, model_width)]
  transfers between devices with their start and end apart: 2 -> 0, of which waited for: 2 -> 0; matrix products, arithmetic and copies ran while one was open for 1% -> 0% of each run, Pallas kernels for 0% -> 0%
where the time goes in v3:
time: 90.8 us; the launch traced here: 90.6 us
  Pallas kernels  89.1 us (98%)
  local copies, waits for them, and re-layouts  1.57 us (2%)
    pallas_call x1, Pallas kernels, shards(): pl.pallas_call(kernel, out_shape=jax.ShapeDtypeStruct((TOK, D), BF16), in...  89.1 us

profile of v3, /device:TPU:1, one launch (start us, length us, event | category | flops | bytes accessed | tf_op | source)
XLA Modules:
  0.0 90.6 jit_solution(13184702692163922903)
XLA Ops:
  0.0 89.1 %shard_map.109 = bf16[16,4096]{1,0:T(8,128)(2,1)} custom-call(bf16[32,128]{1,0:T(8,128)(2,1)} %bitcast.2, s32[8,16]{1,0:T(8,128)} %bitcast.3, bf16[16,4096]{1,0:T(8,128)(2,1)} %hidden_hbm.1, bf16[16,8192]{1,0:T(8,128)(2,1)} %query_hbm.1, bf16[4096,128]{1,0:T(8,128)(2,1)} %router_hbm.1, bf16[16,128,512]{2,1,0:T(8,128)(2,1)} %key_hbm.1, ...), custom_call_target="tpu_custom_call" | custom-call | tf_op jit(solution)/shard_map/pallas_call | solution.py:538
  89.1 1.6 %copy.13 = bf16[16,4096]{1,0:T(8,128)(2,1)} copy(bf16[16,4096]{1,0:T(8,128)(2,1)} %shard_map.109) | data formatting | bytes 262144

commit v4 on v3

--- a/solution.py
+++ b/solution.py
@@ -66,7 +66,7 @@
         pltpu.make_async_copy(self.like, self.like, self.send).wait()
 
 
-N_GROUPS = 11 * PARTS + 11
+N_GROUPS = 10 * PARTS + 18
 N_LOADS = 9
 
 
@@ -108,8 +108,9 @@
         del rest[:count]
         return taken
 
-    att_in, plane_w = take(3), take(3)
-    weight, part1, over_b1, sum1, over_a1 = [take(PARTS) for _ in range(5)]
+    att_in, plane_u, plane_w = take(3), take(3), take(3)
+    scale_out, scale_in = take(2)
+    weight, part1, over_b1, swap_a = [take(PARTS) for _ in range(4)]
     plane, picked, rows, made, back = [take(PARTS) for _ in range(5)]
     part2, over_b2, sum2, over_a2 = [take(PARTS) for _ in range(4)]
     send, recv, local = rest
@@ -138,6 +139,25 @@
     def drain(*copies):
         for copy in copies:
             copy.sent()
+
+    loads = []
+
+    def load(src, dst):
+        copy = pltpu.make_async_copy(src, dst, local.at[len(loads)])
+        copy.start()
+        loads.append(copy)
+        return copy
+
+    query_load, key_load, value_load, ow_load, hidden_load = [
+        load(src, dst)
+        for src, dst in (
+            (query_hbm, query_ref),
+            (key_hbm, key_ref),
+            (value_hbm, value_ref),
+            (ow_hbm, ow_ref),
+            (hidden_hbm, hidden_ref),
+        )
+    ]
 
     barrier = pltpu.get_barrier_semaphore()
     partners = [moved(other=1)]
@@ -146,24 +166,6 @@
             partners += [moved((axis, step)), moved((axis, step), other=1)]
     for partner in partners:
         pl.semaphore_signal(barrier, inc=1, device_id=partner, device_id_type=MESH)
-
-    loads = []
-
-    def load(src, dst):
-        copy = pltpu.make_async_copy(src, dst, local.at[len(loads)])
-        copy.start()
-        loads.append(copy)
-        return copy
-
-    ow_load, query_load, key_load, value_load = [
-        load(src, dst)
-        for src, dst in (
-            (ow_hbm, ow_ref),
-            (query_hbm, query_ref),
-            (key_hbm, key_ref),
-            (value_hbm, value_ref),
-        )
-    ]
 
     row, col = iota((ALL, ALL), 0), iota((ALL, ALL), 1)
     swap = one_hot((row % TOK == col // TOK) & (row // TOK == col % TOK))
@@ -246,6 +248,34 @@
         send_weight(p)
     mid_x[at[0]] = att[at[0]]
     mid_z[at[1]] = att[:, at[1]]
+
+    ids = iota((TOK, EXPERTS), 1)
+    eye = one_hot(iota((TOK, TOK), 0) == iota((TOK, TOK), 1))
+    routes = dot_nt(eye, routes_ref[...].astype(F32).astype(BF16)).astype(jnp.int32)
+    chosen = routes[:, 0:1] == ids
+    for k in range(1, routes.shape[1]):
+        chosen = chosen | (routes[:, k : k + 1] == ids)
+
+    def push_a(r, held):
+        c, a, b = ROT[r]
+        mine = held.at[at[b], at[a]]
+        copies = group(held.at[0, 0:3])
+        for hop in NEAR_FIRST:
+            copies.push(mine, mine, moved((a, hop)))
+        return copies
+
+    def push_b(r, held):
+        c, a, b = ROT[r]
+        mine = held.at[at[b]]
+        copies = group(held.at[0:3])
+        for hop in NEAR_FIRST:
+            copies.push(mine, mine, moved((b, hop)))
+        return copies
+
+    users_a, users_b = [], []
+    for r in range(3):
+        plane_u[r][at[ROT[r][2]], at[ROT[r][1]]] = one_hot(chosen)
+        users_a.append(push_a(r, plane_u[r]))
     att_out = [group(att_in[r].at[0:3]) for r in range(3)]
     over_x.arrived()
     for hop in NEAR_FIRST:
@@ -259,9 +289,12 @@
     att_in[0][at[2]] = mid_z[:, :, at[2]]
     for p in range(PARTS):
         pass_weight(p)
+    for r in range(3):
+        users_a[r].arrived()
+        users_b.append(push_b(r, plane_u[r]))
     for p in range(PARTS):
         hand_over(p)
-    small_loads = [load(hidden_hbm, hidden_ref), load(router_hbm, router_ref)]
+    router_load = load(router_hbm, router_ref)
     expert_loads = [
         load(gate_hbm.at[0], gate_ref),
         load(up_hbm.at[0], up_ref),
@@ -310,56 +343,76 @@
         b_out1.append(scatter_b(p, part1, over_b1))
     drain(over_x, over_z, *weight_near, *weight_far, *twin)
 
-    squares = []
-    rows_a = []
-    a_out1 = [scatter_a(p, b_out1[p], part1, over_b1, sum1, over_a1) for p in range(PARTS)]
+    same = row // TOK == col // TOK
+    names, select, users = [], [], []
+    for r in range(3):
+        c, a, b = ROT[r]
+        users_b[r].arrived()
+        own = at[a] * STRIDE[a] + at[b] * STRIDE[b]
+        slot = iota((ALL, EXPERTS), 0)
+        expert = slot // 64 * STRIDE[c] + slot // 32 % 2 * 64 + own
+        names.append(one_hot(expert == iota((ALL, EXPERTS), 1)))
+        held = plane_u[r][...].reshape(ALL, EXPERTS)
+        uses = dot_nt(names[r], held)
+        rank = dot(uses.astype(BF16), one_hot(same & (row < col)))
+        uses = (uses > 0) & (rank == (row % 2).astype(F32)) & (row // 2 % 16 == col // TOK)
+        select.append(one_hot(uses))
+        uses = dot_nt(held, names[r])
+        rank = dot(one_hot(same & (col < row)), uses.astype(BF16))
+        uses = (uses > 0) & (rank == (col % 2).astype(F32)) & (col // 2 % 16 == row // TOK)
+        users.append(one_hot(uses))
+
+    def exchange(p):
+        c, a, b = ROT[p]
+        b_out1[p].arrived()
+        total = part1[p][at[b]].astype(F32)
+        for i in range(3):
+            total = total + over_b1[p][i].astype(F32)
+        swap_a[p][at[a]] = total.astype(BF16)
+        own = part1[p][at[b], at[a]].astype(F32)
+        for i in range(3):
+            own = own + over_b1[p][i, at[a]].astype(F32)
+        own = own + hidden_ref[:, pl.ds(START[p], WIDE[p])].astype(F32)
+        swap_a[p][at[a], at[a]] = own.astype(BF16)
+        copies = group(swap_a[p].at[0:3])
+        for hop in NEAR_FIRST:
+            copies.push(swap_a[p].at[at[a]], swap_a[p].at[at[a]], moved((a, hop)))
+        return copies
+
+    squares, rows_b = [], []
 
     def finish(p):
         c, a, b = ROT[p]
-        cols = pl.ds(START[p], WIDE[p])
-        held = (hidden_ref[:, cols].astype(F32) + scattered(p, a_out1[p], sum1, over_a1)).astype(
-            BF16
-        )
-        resid[:, cols] = held
-        plane[p][at[b], at[a]] = held
-        mine = plane[p].at[at[b], at[a]]
-        copies = group(plane[p].at[0, 0:3])
-        for hop in NEAR_FIRST:
-            copies.push(mine, mine, moved((a, hop)))
-        rows_a.append(copies)
-        held = held.astype(F32)
-        squares.append(jnp.sum(held * held, axis=-1, keepdims=True))
-
-    def gather_b(p):
-        c, a, b = ROT[p]
-        rows_a[p].arrived()
-        mine = plane[p].at[at[b]]
-        copies = group(plane[p].at[0:3])
-        for hop in NEAR_FIRST:
-            copies.push(mine, mine, moved((b, hop)))
-        return copies
-
-    for copy in small_loads:
-        copy.wait()
+        a_out1[p].arrived()
+        total = swap_a[p][0].astype(F32)
+        for i in range(1, 4):
+            total = total + swap_a[p][i].astype(F32)
+        total = total.astype(BF16).astype(F32)
+        for i in range(0, WIDE[p], 128):
+            j = (START[p] + i) // 128
+            held = total[:, :, i : i + 128] * gain_ref[j : j + 1, :].astype(F32)
+            plane[p][at[b], :, :, i : i + 128] = held.astype(BF16)
+        rows_b.append(push_b(p, plane[p]))
+        own = swap_a[p][0, at[a]].astype(F32)
+        for i in range(1, 4):
+            own = own + swap_a[p][i, at[a]].astype(F32)
+        own = own.astype(BF16)
+        resid[:, pl.ds(START[p], WIDE[p])] = own
+        own = own.astype(F32)
+        squares.append(jnp.sum(own * own, axis=-1, keepdims=True))
+
+    hidden_load.wait()
+    a_out1 = [exchange(p) for p in range(PARTS)]
     for p in range(PARTS):
         finish(p)
-    rows_b = [gather_b(p) for p in range(3)]
+
     scale = lax.rsqrt(sum(squares) * (1.0 / D) + 1e-06)
-
-    def norm(held, scale, i):
-        held = held.astype(F32) * scale * gain_ref[i // 128 : i // 128 + 1, :].astype(F32)
-        return held.astype(BF16)
-
     for i in range(0, D, 128):
-        normed[:, i : i + 128] = norm(resid[:, i : i + 128], scale, i)
-
+        held = resid[:, i : i + 128].astype(F32) * scale
+        held = held * gain_ref[i // 128 : i // 128 + 1, :].astype(F32)
+        normed[:, i : i + 128] = held.astype(BF16)
+    router_load.wait()
     logits = dot(normed[...], router_ref[...])
-    ids = iota((TOK, EXPERTS), 1)
-    eye = one_hot(iota((TOK, TOK), 0) == iota((TOK, TOK), 1))
-    routes = dot_nt(eye, routes_ref[...].astype(F32).astype(BF16)).astype(jnp.int32)
-    chosen = routes[:, 0:1] == ids
-    for k in range(1, routes.shape[1]):
-        chosen = chosen | (routes[:, k : k + 1] == ids)
     top = jnp.max(jnp.where(chosen, logits, -jnp.inf), axis=-1, keepdims=True)
     raised = jnp.where(chosen, jnp.exp(jnp.where(chosen, logits, top) - top), 0.0)
     shares = (raised / jnp.sum(raised, axis=-1, keepdims=True)).astype(BF16)
@@ -368,81 +421,53 @@
     middle = (scale - high).astype(BF16).astype(F32)
     low = scale - high - middle
     scales = jnp.where(lane == 0, high, jnp.where(lane == 1, middle, jnp.where(lane == 2, low, 0.0)))
-    shares_a = []
+    shares_a, shares_b = [], []
     for r in range(3):
         c, a, b = ROT[r]
         plane_w[r][at[b], at[a], :, 0:EXPERTS] = shares
         plane_w[r][at[b], at[a], :, EXPERTS : 2 * EXPERTS] = scales.astype(BF16)
-        mine = plane_w[r].at[at[b], at[a]]
-        copies = group(plane_w[r].at[0, 0:3])
-        for hop in NEAR_FIRST:
-            copies.push(mine, mine, moved((a, hop)))
-        shares_a.append(copies)
-
-    rows_b += [gather_b(p) for p in range(3, PARTS)]
-    shares_b = []
-    for r in range(3):
+        shares_a.append(push_a(r, plane_w[r]))
+
+    def along_line(r, src, dst):
         c, a, b = ROT[r]
-        shares_a[r].arrived()
-        mine = plane_w[r].at[at[b]]
-        copies = group(plane_w[r].at[0:3])
-        for hop in NEAR_FIRST:
-            copies.push(mine, mine, moved((b, hop)))
-        shares_b.append(copies)
-    drain(*att_out, *b_out1, *a_out1, *rows_a, *shares_a)
-
-    same = row // TOK == col // TOK
-    select, combine, scales = [], [], []
-    for r in range(3):
-        c, a, b = ROT[r]
-        shares_b[r].arrived()
-        own = at[a] * STRIDE[a] + at[b] * STRIDE[b]
-
-        def expert(slot):
-            return slot // 64 * STRIDE[c] + slot // 32 % 2 * 64 + own
-
-        held = plane_w[r][...].reshape(ALL, 2 * EXPERTS)
-        scales.append(jnp.sum(held[:, EXPERTS:].astype(F32), axis=-1, keepdims=True))
-        held = held[:, :EXPERTS]
-        names = one_hot(expert(iota((ALL, EXPERTS), 0)) == iota((ALL, EXPERTS), 1))
-        share = dot_nt(names, held)
-        uses = share > 0
-        rank = dot(one_hot(uses), one_hot(same & (row < col)))
-        uses = uses & (rank == (row % 2).astype(F32)) & (row // 2 % 16 == col // TOK)
-        select.append(one_hot(uses))
-        share = dot_nt(held, names)
-        uses = share > 0
-        rank = dot(one_hot(same & (col < row)), one_hot(uses))
-        uses = uses & (rank == (col % 2).astype(F32)) & (col // 2 % 16 == row // TOK)
-        combine.append(jnp.where(uses, share, 0.0).astype(BF16))
-
-    def along_line(p, src, dst):
-        c, a, b = ROT[p]
-        copies = group(src[p].at[0:7])
+        copies = group(src.at[0:7])
         for step in (1, 3, 5, 7, 2, 6, 4):
             step_p, step_c = step // 4, step % 4
             there = plus(c, step_c) * 2 + lax.rem(pool + step_p, 2)
             copies.push(
-                src[p].at[there], dst[p].at[at[c] * 2 + pool], moved((c, step_c), other=step_p)
+                src.at[there], dst.at[at[c] * 2 + pool], moved((c, step_c), other=step_p)
             )
-        dst[p][at[c] * 2 + pool] = src[p][at[c] * 2 + pool]
+        dst[at[c] * 2 + pool] = src[at[c] * 2 + pool]
         return copies
 
     line_out = []
-    for p in range(PARTS):
+
+    def pick(p):
         rows_b[p].arrived()
-        held = plane[p][...].reshape(ALL, WIDE[p])
-        held = jnp.concatenate(
-            [
-                norm(held[:, i : i + 128], scales[p % 3], START[p] + i)
-                for i in range(0, WIDE[p], 128)
-            ],
-            axis=1,
-        )
-        outgoing = dot(select[p % 3], held).astype(BF16)
+        outgoing = dot(select[p % 3], plane[p][...].reshape(ALL, WIDE[p])).astype(BF16)
         picked[p][...] = outgoing.reshape(8, 32, WIDE[p])
-        line_out.append(along_line(p, picked, rows))
-    drain(*rows_b, *shares_b)
+        line_out.append(along_line(p, picked[p], rows[p]))
+
+    for p in range(3):
+        pick(p)
+    for r in range(3):
+        shares_a[r].arrived()
+        shares_b.append(push_b(r, plane_w[r]))
+    for p in range(3, PARTS):
+        pick(p)
+    shares_b[0].arrived()
+    held = plane_w[0][...].reshape(ALL, 2 * EXPERTS)[:, EXPERTS:]
+    scale_out[...] = dot(select[0], held).astype(BF16).reshape(8, 32, EXPERTS)
+    scale_line = along_line(0, scale_out, scale_in)
+    combine = []
+    for r in range(3):
+        if r:
+            shares_b[r].arrived()
+        held = plane_w[r][...].reshape(ALL, 2 * EXPERTS)[:, :EXPERTS]
+        share = dot_nt(held, names[r])
+        combine.append(jnp.where(users[r] > 0, share, 0.0).astype(BF16))
+    drain(*att_out, *users_a, *users_b, *b_out1, *a_out1)
+    drain(*rows_b, *shares_a, *shares_b)
 
     for copy in expert_loads:
         copy.wait()
@@ -466,8 +491,10 @@
             gate, up = gate_acc[...] + gate, up_acc[...] + up
         gate_acc[...] = gate
         up_acc[...] = up
-    gate = gate_acc[...]
-    activated = (gate / (1.0 + jnp.exp(-gate)) * up_acc[...]).astype(BF16)
+    scale_line.arrived()
+    scale = jnp.sum(scale_in[...].reshape(ALL, EXPERTS).astype(F32), axis=-1, keepdims=True)
+    gate = gate_acc[...] * scale
+    activated = (gate / (1.0 + jnp.exp(-gate)) * (up_acc[...] * scale)).astype(BF16)
     activated = [activated] + [
         dot(one_hot(place(col, r) == row), activated).astype(BF16) for r in (1, 2)
     ]
@@ -475,8 +502,8 @@
     for p in range(PARTS):
         result = dot(activated[p % 3], down_ref[:, pl.ds(START[p], WIDE[p])]).astype(BF16)
         made[p][...] = result.reshape(8, 32, WIDE[p])
-        line_back.append(along_line(p, made, back))
-    drain(*line_out)
+        line_back.append(along_line(p, made[p], back[p]))
+    drain(scale_line, *line_out)
 
     b_out2 = []
     for p in range(PARTS):
@@ -516,12 +543,13 @@
         pltpu.VMEM((ALL, HID), F32),
         pltpu.VMEM((ALL, HID), F32),
         *[pltpu.VMEM((4, 4, 4, TOK, HD), BF16)] * 3,
+        *[pltpu.VMEM((4, 4, TOK, EXPERTS), BF16)] * 3,
         *[pltpu.VMEM((4, 4, TOK, 2 * EXPERTS), BF16)] * 3,
+        *[pltpu.VMEM((8, 32, EXPERTS), BF16)] * 2,
         *parts(4, HD),
         *parts(4, 4, TOK),
         *parts(3, 4, TOK),
-        *parts(4, TOK),
-        *parts(3, TOK),
+        *parts(4, 4, TOK),
         *parts(4, 4, TOK),
         *parts(8, 32),
         *parts(8, 32),

time: 90.8 us -> 89.1 us (0.981)
  Pallas kernels: 89.1 us -> 87 us
    pallas_call x1, Pallas kernels: 89.1 us -> 87 us  [shards(): pl.pallas_call(kernel, out_shape=jax.ShapeDtypeStruct((TOK, D), BF16), in...]
where the time goes in v4:
time: 89.1 us; the launch traced here: 88.6 us
  Pallas kernels  87 us (98%)
  local copies, waits for them, and re-layouts  1.57 us (2%)
    pallas_call x1, Pallas kernels, shards(): pl.pallas_call(kernel, out_shape=jax.ShapeDtypeStruct((TOK, D), BF16), in...  87 us

profile of v4, /device:TPU:1, one launch (start us, length us, event | category | flops | bytes accessed | tf_op | source)
XLA Modules:
  0.0 88.6 jit_solution(11857915276980818583)
XLA Ops:
  0.0 87.0 %shard_map.109 = bf16[16,4096]{1,0:T(8,128)(2,1)} custom-call(bf16[32,128]{1,0:T(8,128)(2,1)} %bitcast.2, s32[8,16]{1,0:T(8,128)} %bitcast.3, bf16[16,4096]{1,0:T(8,128)(2,1)} %hidden_hbm.1, bf16[16,8192]{1,0:T(8,128)(2,1)} %query_hbm.1, bf16[4096,128]{1,0:T(8,128)(2,1)} %router_hbm.1, bf16[16,128,512]{2,1,0:T(8,128)(2,1)} %key_hbm.1, ...), custom_call_target="tpu_custom_call" | custom-call | tf_op jit(solution)/shard_map/pallas_call | solution.py:566
  87.0 1.6 %copy.13 = bf16[16,4096]{1,0:T(8,128)(2,1)} copy(bf16[16,4096]{1,0:T(8,128)(2,1)} %shard_map.109) | data formatting | bytes 262144

commit v5 on v4

--- a/solution.py
+++ b/solution.py
@@ -66,7 +66,7 @@
         pltpu.make_async_copy(self.like, self.like, self.send).wait()
 
 
-N_GROUPS = 10 * PARTS + 18
+N_GROUPS = 10 * PARTS + 20
 N_LOADS = 9
 
 
@@ -109,7 +109,7 @@
         return taken
 
     att_in, plane_u, plane_w = take(3), take(3), take(3)
-    scale_out, scale_in = take(2)
+    plane_s, scale_out, scale_in = take(3)
     weight, part1, over_b1, swap_a = [take(PARTS) for _ in range(4)]
     plane, picked, rows, made, back = [take(PARTS) for _ in range(5)]
     part2, over_b2, sum2, over_a2 = [take(PARTS) for _ in range(4)]
@@ -407,6 +407,13 @@
         finish(p)
 
     scale = lax.rsqrt(sum(squares) * (1.0 / D) + 1e-06)
+    lane = iota((TOK, EXPERTS), 1)
+    high = scale.astype(BF16).astype(F32)
+    middle = (scale - high).astype(BF16).astype(F32)
+    low = scale - high - middle
+    scales = jnp.where(lane == 0, high, jnp.where(lane == 1, middle, jnp.where(lane == 2, low, 0.0)))
+    plane_s[at[ROT[0][2]], at[ROT[0][1]]] = scales.astype(BF16)
+    scale_a = push_a(0, plane_s)
     for i in range(0, D, 128):
         held = resid[:, i : i + 128].astype(F32) * scale
         held = held * gain_ref[i // 128 : i // 128 + 1, :].astype(F32)
@@ -416,16 +423,10 @@
     top = jnp.max(jnp.where(chosen, logits, -jnp.inf), axis=-1, keepdims=True)
     raised = jnp.where(chosen, jnp.exp(jnp.where(chosen, logits, top) - top), 0.0)
     shares = (raised / jnp.sum(raised, axis=-1, keepdims=True)).astype(BF16)
-    lane = iota((TOK, EXPERTS), 1)
-    high = scale.astype(BF16).astype(F32)
-    middle = (scale - high).astype(BF16).astype(F32)
-    low = scale - high - middle
-    scales = jnp.where(lane == 0, high, jnp.where(lane == 1, middle, jnp.where(lane == 2, low, 0.0)))
     shares_a, shares_b = [], []
     for r in range(3):
         c, a, b = ROT[r]
-        plane_w[r][at[b], at[a], :, 0:EXPERTS] = shares
-        plane_w[r][at[b], at[a], :, EXPERTS : 2 * EXPERTS] = scales.astype(BF16)
+        plane_w[r][at[b], at[a]] = shares
         shares_a.append(push_a(r, plane_w[r]))
 
     def along_line(r, src, dst):
@@ -450,24 +451,25 @@
 
     for p in range(3):
         pick(p)
+    scale_a.arrived()
+    scale_b = push_b(0, plane_s)
     for r in range(3):
         shares_a[r].arrived()
         shares_b.append(push_b(r, plane_w[r]))
     for p in range(3, PARTS):
         pick(p)
-    shares_b[0].arrived()
-    held = plane_w[0][...].reshape(ALL, 2 * EXPERTS)[:, EXPERTS:]
+    scale_b.arrived()
+    held = plane_s[...].reshape(ALL, EXPERTS)
     scale_out[...] = dot(select[0], held).astype(BF16).reshape(8, 32, EXPERTS)
     scale_line = along_line(0, scale_out, scale_in)
     combine = []
     for r in range(3):
-        if r:
-            shares_b[r].arrived()
-        held = plane_w[r][...].reshape(ALL, 2 * EXPERTS)[:, :EXPERTS]
+        shares_b[r].arrived()
+        held = plane_w[r][...].reshape(ALL, EXPERTS)
         share = dot_nt(held, names[r])
         combine.append(jnp.where(users[r] > 0, share, 0.0).astype(BF16))
     drain(*att_out, *users_a, *users_b, *b_out1, *a_out1)
-    drain(*rows_b, *shares_a, *shares_b)
+    drain(*rows_b, scale_a, scale_b, *shares_a, *shares_b)
 
     for copy in expert_loads:
         copy.wait()
@@ -544,7 +546,7 @@
         pltpu.VMEM((ALL, HID), F32),
         *[pltpu.VMEM((4, 4, 4, TOK, HD), BF16)] * 3,
         *[pltpu.VMEM((4, 4, TOK, EXPERTS), BF16)] * 3,
-        *[pltpu.VMEM((4, 4, TOK, 2 * EXPERTS), BF16)] * 3,
+        *[pltpu.VMEM((4, 4, TOK, EXPERTS), BF16)] * 4,
         *[pltpu.VMEM((8, 32, EXPERTS), BF16)] * 2,
         *parts(4, HD),
         *parts(4, 4, TOK),

time: 89.1 us -> 88.3 us (level)
  no operation moved by 1% of the time
where the time goes in v5:
time: 88.3 us; the launch traced here: 87.8 us
  Pallas kernels  86.3 us (98%)
  local copies, waits for them, and re-layouts  1.57 us (2%)
    pallas_call x1, Pallas kernels, shards(): pl.pallas_call(kernel, out_shape=jax.ShapeDtypeStruct((TOK, D), BF16), in...  86.3 us

profile of v5, /device:TPU:1, one launch (start us, length us, event | category | flops | bytes accessed | tf_op | source)
XLA Modules:
  0.0 87.8 jit_solution(13701276357310449000)
XLA Ops:
  0.0 86.3 %shard_map.109 = bf16[16,4096]{1,0:T(8,128)(2,1)} custom-call(bf16[32,128]{1,0:T(8,128)(2,1)} %bitcast.2, s32[8,16]{1,0:T(8,128)} %bitcast.3, bf16[16,4096]{1,0:T(8,128)(2,1)} %hidden_hbm.1, bf16[16,8192]{1,0:T(8,128)(2,1)} %query_hbm.1, bf16[4096,128]{1,0:T(8,128)(2,1)} %router_hbm.1, bf16[16,128,512]{2,1,0:T(8,128)(2,1)} %key_hbm.1, ...), custom_call_target="tpu_custom_call" | custom-call | tf_op jit(solution)/shard_map/pallas_call | solution.py:568
  86.3 1.6 %copy.13 = bf16[16,4096]{1,0:T(8,128)(2,1)} copy(bf16[16,4096]{1,0:T(8,128)(2,1)} %shard_map.109) | data formatting | bytes 262144
